TPU v7x, 128 devices: a whole 4x4x4 slice. The times are simulated.
128 devices in a mesh: row: 8 (over y, core), col: 16 (over z, x).
Axes of the slice: x: 4, y: 4, z: 4, core: 2. Of those that a mesh axis runs over, the one named last changes fastest.
Arguments:
- edge_feats: bfloat16 [262144, 128], P(('row', 'col')), may hold values from -6 to 6
- edge_rows: int32 [262144], P(('row', 'col')), may hold values from 0 to 4095, as said below
- edge_cols: int32 [262144], P(('row', 'col')), may hold values from 0 to 511, as said below
- w_in: bfloat16 [128, 512], replicated, may hold values from -0.5 to 0.5
- w_mid: bfloat16 [512, 512], replicated, may hold values from -0.25 to 0.25
- w_out: bfloat16 [512, 256], replicated, may hold values from -0.25 to 0.25
- cholesky_panel: bfloat16 [65536, 512], P(('row', 'col')), may hold values from -0.375 to 0.375
- diag_inverse: float32 [2, 256, 256], replicated, as said below
Outputs:
- reduced: float32 [65536, 8192], P('row', 'col')
Inputs may be any that keep to these rules, and one draw needn't show every extreme that they name: `edge_rows`: on each device the edges are grouped by the device that owns their block: edges d * 16 to (d + 1) * 16 - 1 of a device have their row slot within the row slots of row index d // 16, each row index holding 512 slots in order. `edge_cols`: likewise edges d * 16 to (d + 1) * 16 - 1 have their column slot within the 32 slots of col index d % 16. `diag_inverse`: each block is lower triangular with a positive diagonal.
All inputs are finite; a program needn't handle non-finite values.
Results may differ from a plain program's by a relative error of at most 0.0053.
Values may be sent and summed in bfloat16 or wider, within the bound.
No kernel may reach another device: no remote copies, remote signals or barrier semaphores. Data moves between devices by JAX's collectives and lax.ppermute only.
A program may use at most 448 MiB of HBM per device.

v0:
```python
import jax
import jax.numpy as jnp
from jax import lax
from jax.sharding import PartitionSpec as P

TILE = 16
BLOCK = 256
STEPS = 2
SLAB_DEV = 512


def from_root(block, axis, owner):
    block = jnp.where(lax.axis_index(axis) == owner, block, jnp.zeros_like(block))
    return lax.psum(block, axis)


def edge_network(feats, w_in, w_mid, w_out):
    hidden_one = jax.nn.silu(jnp.dot(feats, w_in, preferred_element_type=jnp.float32)).astype(
        jnp.bfloat16
    )
    hidden_two = jax.nn.silu(jnp.dot(hidden_one, w_mid, preferred_element_type=jnp.float32)).astype(
        jnp.bfloat16
    )
    return jnp.dot(hidden_two, w_out, preferred_element_type=jnp.float32)


def body(edge_feats, edge_rows, edge_cols, w_in, w_mid, w_out, cholesky_panel, diag_inverse):
    n_row = lax.axis_size("row")
    n_col = lax.axis_size("col")
    panel_local = cholesky_panel.shape[0]
    rows_dev = panel_local * n_col
    row_slots = rows_dev // TILE
    col_slots = SLAB_DEV // TILE
    per_peer = edge_feats.shape[0] // (n_row * n_col)
    tile_size = TILE * TILE
    full_panel = lax.all_gather(cholesky_panel, "col", axis=0, tiled=True)
    target = edge_rows % row_slots * col_slots + edge_cols % col_slots
    tile_values = edge_network(edge_feats, w_in, w_mid, w_out)
    received, placed = (
        lax.all_to_all(
            tile_values.reshape(n_row * n_col, per_peer, tile_size),
            ("row", "col"),
            split_axis=0,
            concat_axis=0,
            tiled=True,
        ),
        lax.all_to_all(
            target.reshape(n_row * n_col, per_peer),
            ("row", "col"),
            split_axis=0,
            concat_axis=0,
            tiled=True,
        ),
    )
    flat_place = placed.reshape(-1)
    assembled = jnp.zeros((row_slots * col_slots, tile_size), jnp.float32)
    assembled = assembled.at[flat_place].add(received.reshape(-1, tile_size))
    hamiltonian = (
        assembled.reshape(row_slots, col_slots, TILE, TILE)
        .transpose(0, 2, 1, 3)
        .reshape(rows_dev, SLAB_DEV)
    )
    row_pos = lax.axis_index("row")
    for block_step in range(STEPS):
        low = block_step * BLOCK
        high = low + BLOCK
        solved = jnp.dot(
            diag_inverse[block_step],
            hamiltonian[low:high],
            precision=lax.Precision.HIGHEST,
            preferred_element_type=jnp.float32,
        )
        solved_b = from_root(solved.astype(jnp.bfloat16), "row", 0)
        update = jnp.dot(full_panel[:, low:high], solved_b, preferred_element_type=jnp.float32)
        updated = hamiltonian - update
        first_head = jnp.concatenate([hamiltonian[:low], solved], axis=0)
        head_rows = jnp.where(row_pos == 0, first_head, updated[:high])
        hamiltonian = lax.dynamic_update_slice_in_dim(updated, head_rows, 0, 0)
    return hamiltonian


def solution(mesh):
    return jax.shard_map(
        body,
        mesh=mesh,
        in_specs=(
            P(("row", "col"), None),
            P(("row", "col")),
            P(("row", "col")),
            P(),
            P(),
            P(),
            P(("row", "col"), None),
            P(),
        ),
        out_specs=P("row", "col"),
        check_vma=False,
    )
```

profile of v0, /device:TPU:0, one launch (start us, length us, event | category | flops | bytes accessed | tf_op | source)
XLA Modules:
  0.0 453.7 jit_solution(13340831778597191293)
XLA Ops:
  7.4 0.8 fusion.14
  8.2 0.7 all_to_all.9
  8.9 11.1 %all-to-all-start = ((s32[128,1,16]{2,1,0:T(1,128)}), s32[128,1,16]{2,1,0:T(1,128)S(1)}, u32[]{:S(2)}, u32[]{:S(2)}) async-start(s32[128,1,16]{2,1,0:T(1,128)} %bitcast), calls=%async_computation | async-start | bytes 131072 | tf_op jit(solution)/shard_map/all_to_all | solution.py:47
  20.0 5.3 %fusion.5 = f32[2048,512]{1,0:T(8,128)} fusion(bf16[512,512]{1,0:T(8,128)(2,1)S(1)} %copy-done, bf16[2048,128]{1,0:T(8,128)(2,1)} %param.8, bf16[128,512]{1,0:T(8,128)(2,1)} %param.11), kind=kOutput, calls=%fused_computation.10 | convolution fusion | flops 1347420160 | bytes 5373952 | tf_op jit(solution)/shard_map/dot_general | solution.py:21
  25.4 4.8 %fusion.4 = f32[2048,256]{1,0:T(8,128)} fusion(bf16[512,256]{1,0:T(8,128)(2,1)S(1)} %copy-done.3, f32[2048,512]{1,0:T(8,128)} %fusion.5), kind=kOutput, calls=%fused_computation.9 | convolution fusion | flops 542113792 | bytes 6553600 | tf_op jit(solution)/shard_map/dot_general | solution.py:24
  30.1 9.8 %all-to-all-start.1 = ((f32[128,16,256]{2,1,0:T(8,128)}), f32[128,16,256]{2,1,0:T(8,128)S(1)}, u32[]{:S(2)}, u32[]{:S(2)}) async-start(f32[128,16,256]{2,1,0:T(8,128)} %bitcast.2), calls=%async_computation.1 | async-start | bytes 4194304 | tf_op jit(solution)/shard_map/all_to_all | solution.py:40
  40.5 0.8 reduce.3
  41.4 28.2 %all-to-all-done.1 = f32[128,16,256]{2,1,0:T(8,128)S(1)} async-done(((f32[128,16,256]{2,1,0:T(8,128)}), f32[128,16,256]{2,1,0:T(8,128)S(1)}, u32[]{:S(2)}, u32[]{:S(2)}) %all-to-all-start.1) | async-done | bytes 2097184 | tf_op jit(solution)/shard_map/all_to_all | solution.py:40
  69.6 18.7 %scatter_custom_fusion = f32[16384,256]{1,0:T(8,128)} fusion(s32[2048]{0:T(1024)S(1)} %bitcast.37, f32[2048,256]{1,0:T(8,128)S(1)} %bitcast.36, f32[]{:T(128)} %constant.34.clone.1), kind=kCustom, calls=%fused_computation.3 | custom fusion | flops 524288 | bytes 16777220 | tf_op jit(solution)/shard_map/scatter-add | solution.py:57
  88.3 17.4 %copy.22 = f32[16384,256]{0,1:T(8,128)} copy(f32[16384,256]{1,0:T(8,128)} %scatter_custom_fusion) | data formatting | bytes 33554432 | tf_op jit(solution)/shard_map/scatter-add | solution.py:57
  105.8 38.7 %reshape.52 = f32[512,32,16,16]{1,0,3,2:T(8,128)} reshape(f32[16384,256]{0,1:T(8,128)} %copy.22) | data formatting | bytes 33554432 | tf_op jit(solution)/shard_map/reshape | solution.py:59
  144.4 1.8 slice.38
  146.3 2.8 copy.24
  149.1 4.5 slice.29
  153.6 1.4 convert_select_fusion.1
  155.1 0.5 all-gather.2.cloned.1.call-update
  155.6 88.5 %copy.23 = f32[512,16,32,16]{3,2,1,0:T(8,128)} copy(f32[512,16,32,16]{2,0,3,1:T(8,128)} %bitcast.4) | data formatting | bytes 33554432 | tf_op jit(solution)/shard_map/transpose | solution.py:60
  244.1 106.9 %reshape.53 = f32[8192,512]{1,0:T(8,128)} reshape(f32[512,16,32,16]{3,2,1,0:T(8,128)} %copy.23) | data formatting | bytes 33554432 | tf_op jit(solution)/shard_map/reshape | solution.py:61
  351.0 15.6 %bitcast_subtract_fusion.1 = f32[8192,512]{1,0:T(8,128)} fusion(f32[8192,512]{1,0:T(8,128)} %reshape.53, bf16[256,512]{1,0:T(8,128)(2,1)} %all-reduce.3.cloned.1.call-done, bf16[8192,512]{1,0:T(8,128)(2,1)} %all-gather.2.cloned.1.call-done), kind=kOutput, calls=%fused_computation.2 | convolution fusion | flops 2151677952 | bytes 38010880 | tf_op jit(solution)/shard_map/dot_general | solution.py:74
  366.7 1.9 constant_dynamic-update-slice_fusion
  368.6 2.4 convert_select_fusion
  371.0 57.1 %all-reduce.5.cloned.1.call-done = bf16[256,512]{1,0:T(8,128)(2,1)} async-done(((bf16[256,512]{1,0:T(8,128)(2,1)}), bf16[256,512]{1,0:T(8,128)(2,1)}) %all-reduce.5.cloned.1.call-update) | async-done | bytes 262160 | tf_op jit(solution)/shard_map/psum | solution.py:14
  428.2 15.7 %bitcast_subtract_fusion = f32[8192,512]{1,0:T(8,128)} fusion(f32[8192,512]{1,0:T(8,128)} %get-tuple-element.5, bf16[256,512]{1,0:T(8,128)(2,1)} %all-reduce.5.cloned.1.call-done, bf16[8192,512]{1,0:T(8,128)(2,1)} %all-gather.2.cloned.1.call-done), kind=kOutput, calls=%fused_computation.1 | convolution fusion | flops 2151677952 | bytes 38010880 | tf_op jit(solution)/shard_map/dot_general | solution.py:74
  443.9 2.4 fusion.6
  (19 shorter events, 0.8 us)
Async XLA Ops:
  7.4 12.6 %copy-start = (bf16[512,512]{1,0:T(8,128)(2,1)S(1)}, bf16[512,512]{1,0:T(8,128)(2,1)}, u32[]{:S(2)}) copy-start(bf16[512,512]{1,0:T(8,128)(2,1)} %param.12) | copy-start | bytes 1572868
  8.9 21.3 %all-to-all-start = ((s32[128,1,16]{2,1,0:T(1,128)}), s32[128,1,16]{2,1,0:T(1,128)S(1)}, u32[]{:S(2)}, u32[]{:S(2)}) async-start(s32[128,1,16]{2,1,0:T(1,128)} %bitcast), calls=%async_computation | async-start | bytes 131072 | tf_op jit(solution)/shard_map/all_to_all | solution.py:47
  20.0 5.3 %copy-start.3 = (bf16[512,256]{1,0:T(8,128)(2,1)S(1)}, bf16[512,256]{1,0:T(8,128)(2,1)}, u32[]{:S(2)}) copy-start(bf16[512,256]{1,0:T(8,128)(2,1)} %param.13) | copy-start | bytes 786436
  30.1 39.5 %all-to-all-start.1 = ((f32[128,16,256]{2,1,0:T(8,128)}), f32[128,16,256]{2,1,0:T(8,128)S(1)}, u32[]{:S(2)}, u32[]{:S(2)}) async-start(f32[128,16,256]{2,1,0:T(8,128)} %bitcast.2), calls=%async_computation.1 | async-start | bytes 4194304 | tf_op jit(solution)/shard_map/all_to_all | solution.py:40
  39.9 311.1 %all-reduce.3.cloned.1.call-start = ((), (), s32[]{:S(2)}) async-start(), calls=%async_computation.2 | async-start | bytes 524288 | tf_op jit(solution)/shard_map/psum | solution.py:14
  146.3 7.3 %copy-start.2 = (f32[2,256,256]{2,1,0:T(8,128)S(1)}, f32[2,256,256]{2,1,0:T(8,128)}, u32[]{:S(2)}) copy-start(f32[2,256,256]{2,1,0:T(8,128)} %param.15) | copy-start | bytes 1572868
  155.0 196.0 %all-gather.2.cloned.1.call-start = ((), (), s32[]{:S(2)}) async-start(), calls=%async_computation.3 | async-start | bytes 8912896 | tf_op jit(solution)/shard_map/all_gather | solution.py:36
  155.6 272.6 %all-reduce.5.cloned.1.call-start = ((), (), s32[]{:S(2)}) async-start(), calls=%async_computation.4 | async-start | bytes 524288 | tf_op jit(solution)/shard_map/psum | solution.py:14
  428.2 18.1 %copy-start.1 = (bf16[512,512]{1,0:T(8,128)(2,1)S(1)}, bf16[512,512]{1,0:T(8,128)(2,1)}, u32[]{:S(2)}) copy-start(bf16[512,512]{1,0:T(8,128)(2,1)} %param.12) | copy-start | bytes 1572868
Sparse Core Ops, SparseCore 0:
  155.1 57.0 all-reduce.2
  371.1 56.9 all-reduce.4
Sparse Core Ops, SparseCore 1:
  157.8 66.7 all-gather.1
where the time goes:
time: 460 us; the launch traced here: 454 us
  local copies, waits for them, and re-layouts  262 us (57%)
  waiting for transfers between devices  85.9 us (19%)
  matrix products  45.2 us (10%)
  other arithmetic  24.7 us (5%)
  starting transfers between devices  21 us (5%)
  between operations  15 us (3%)
    reshape x1, local copies, waits for them, and re-layouts, body(): hamiltonian = assembled.reshape(row_slots, col_slots, TILE, TILE).transpo...  107 us
    transpose x1, local copies, waits for them, and re-layouts, body(): hamiltonian = assembled.reshape(row_slots, col_slots, TILE, TILE).transpo...  88.5 us
    psum x2, waiting for transfers between devices, from_root(): return lax.psum(block, axis)  57.2 us
    reshape x1, local copies, waits for them, and re-layouts, body(): assembled.reshape(row_slots, col_slots, TILE, TILE).transpose(0, 2, 1, 3)  38.7 us
    dot_general x2, matrix products, body(): jnp.dot(full_panel[:, low:high], solved_b, preferred_element_type=jnp.flo...  31.3 us
    all_to_all x1, waiting for transfers between devices, body(): lax.all_to_all(tile_values.reshape(n_row * n_col, per_peer, tile_size), (...  28.2 us
    scatter-add x1, other arithmetic, body(): assembled = assembled.at[flat_place].add(received.reshape(-1, tile_size))  18.7 us
    scatter-add x1, local copies, waits for them, and re-layouts, body(): assembled = assembled.at[flat_place].add(received.reshape(-1, tile_size))  17.4 us
  transfers between devices with their start and end apart: 5, of which 2 were waited for; matrix products, arithmetic and copies ran while one was open for 46% of the time, Pallas kernels for 0%

commit v1 on v0

v1 whole, which is shorter than its diff:
```python
import jax
import jax.numpy as jnp
from jax import lax
from jax.experimental import pallas as pl
from jax.experimental.pallas import tpu as pltpu
from jax.sharding import PartitionSpec as P

TILE = 16
BLOCK = 256
HEAD = 512
LANES = 128
GROUP = 8
CHUNK = 256
SET = 16
PASS = 256
PAYLOAD = 40
MIB = 1024 * 1024
F32 = jnp.float32
BF16 = jnp.bfloat16


def dot(a, b, precision=None):
    return jnp.dot(a, b, precision=precision, preferred_element_type=F32)


def dot_t(a, b):
    return lax.dot_general(a, b, (((1,), (1,)), ((), ())), preferred_element_type=F32)


def silu(v):
    half = 0.5 * v
    return half + half * jnp.tanh(half)


def hidden(feats, w_in, w_mid):
    one = silu(dot(feats, w_in)).astype(BF16)
    return silu(dot(one, w_mid)).astype(BF16)


def iota(shape, dim):
    return lax.broadcasted_iota(jnp.int32, shape, dim)


def head_rows(code_ref, recv_ref, w_in, w_mid, w_tile, head, sums):
    code = code_ref[...]
    slot = code // 32
    column = code % 32
    groups = code.shape[0]
    keep = slot < HEAD // TILE
    ones = jnp.where(keep, 1.0, 0.0).astype(F32)
    upto = jnp.where(iota((LANES, LANES), 0) <= iota((LANES, LANES), 1), 1.0, 0.0).astype(BF16)
    before = jnp.where(iota((groups, groups), 1) < iota((groups, groups), 0), 1.0, 0.0).astype(BF16)
    totals = jnp.broadcast_to(jnp.sum(ones, axis=1, keepdims=True), ones.shape)
    place = dot(ones.astype(BF16), upto) + dot(before, totals.astype(BF16)) - 1.0
    place = jnp.where(keep, place, -1.0)
    count = jnp.sum(ones).astype(jnp.int32)
    slot_f = slot.astype(F32)
    column_f = column.astype(F32)
    sums[...] = jnp.zeros_like(sums)

    def one_pass(step, carry):
        wanted = (iota((PASS, LANES), 0) + step * PASS).astype(F32)
        feats = jnp.zeros((PASS, LANES), F32)
        by_row = jnp.zeros((16, PASS), F32)
        by_col = jnp.zeros((PASS, 16), F32)
        which = iota((16, LANES), 0)
        for g in range(groups):
            pick = jnp.where(place[g : g + 1, :] == wanted, 1.0, 0.0).astype(BF16)
            block = recv_ref[g * 8 : (g + 1) * 8, 16:32, :].reshape(LANES, LANES)
            feats += dot(pick, block)
            where_to = jnp.where(
                which == 0, slot_f[g : g + 1, :], jnp.where(which == 1, column_f[g : g + 1, :], 0.0)
            ).astype(BF16)
            by_row += dot_t(where_to, pick)
            by_col += dot_t(pick, where_to)
        two = hidden(feats.astype(BF16), w_in[...], w_mid[...])
        col_c = by_col[:, 1:2].astype(jnp.int32)
        mask = iota((PASS, 2 * LANES), 1) % LANES // TILE == col_c % GROUP
        row_c = by_row[1:2, :].astype(jnp.int32)
        key = row_c // GROUP * (HEAD // TILE) + by_row[0:1, :].astype(jnp.int32)
        spread = jnp.where(iota((LANES, PASS), 0) == key, 1.0, 0.0).astype(F32)
        for j in range(TILE // 2):
            lanes = slice(j * 2 * LANES, (j + 1) * 2 * LANES)
            values = jnp.where(mask, dot(two, w_tile[:, lanes]), 0.0)
            sums[:, lanes] += dot(spread, values, lax.Precision.HIGHEST)
        return carry

    lax.fori_loop(0, (count + PASS - 1) // PASS, one_pass, 0)
    per = HEAD // TILE
    for a in range(TILE):
        for q in range(HEAD // LANES):
            head[pl.ds(q * HEAD + a, per, stride=TILE), :] = sums[
                q * per : (q + 1) * per, a * LANES : (a + 1) * LANES
            ]


def some(bits):
    return bits != 0


def low_bit(bits):
    low = bits & -bits
    place = 0
    for width, mask in ((8, 0xFF00), (4, 0xF0F0), (2, 0xCCCC), (1, 0xAAAA)):
        place = place + jnp.where((low & mask) != 0, width, 0)
    return place


def assemble_kernel(dest, lost, clashes, code_ref, recv_ref, lane_ref, w_in, w_mid, w_tile, slab, head, tiles, sums):
    peers = CHUNK // SET

    def clear(i, carry):
        slab[pl.ds(pl.multiple_of(i * 512, 512), 512), :] = jnp.zeros((512, LANES), F32)
        return carry

    lax.fori_loop(0, slab.shape[0] // 512, clear, 0)

    def chunk(k, carry):
        start = pl.multiple_of(k * peers, peers)
        feats = recv_ref[pl.ds(start, peers), 0:16, :].reshape(CHUNK, LANES)
        two = hidden(feats, w_in[...], w_mid[...])
        lane = lane_ref[pl.ds(start, peers), :]
        lane = jnp.broadcast_to(lane[:, None, :], (peers, 16, 16)).reshape(CHUNK, 16)
        own = iota((CHUNK, 16), 0) % 16 == iota((CHUNK, 16), 1)
        lane = jnp.sum(jnp.where(own, lane, 0.0), axis=1, keepdims=True).astype(jnp.int32)
        mask = iota((CHUNK, LANES), 1) // TILE == lane
        for j in range(TILE // 2):
            pair = dot(two, w_tile[:, j * 2 * LANES : (j + 1) * 2 * LANES])
            for i in range(2):
                tiles[pl.ds(2 * j + i, CHUNK, stride=TILE), :] = jnp.where(
                    mask, pair[:, i * LANES : (i + 1) * LANES], 0.0
                )

        def load(e):
            return tiles[pl.ds(pl.multiple_of(e * TILE, TILE), TILE), :]

        def place(i, inner):
            at = [pl.multiple_of(dest[k * CHUNK + i * SET + e], TILE) for e in range(SET)]
            sums = [slab[pl.ds(at[e], TILE), :] + load(i * SET + e) for e in range(SET)]
            for e in range(SET):
                slab[pl.ds(at[e], TILE), :] = sums[e]
            return inner

        def repair(bits):
            peer = low_bit(bits)

            def one(left):
                e = peer * SET + low_bit(left)
                at = pl.multiple_of(dest[k * CHUNK + e], TILE)
                slab[pl.ds(at, TILE), :] += load(e)
                return left & (left - 1)

            lax.while_loop(some, one, lost[k * peers + peer])
            return bits & (bits - 1)

        lax.fori_loop(0, CHUNK // SET, place, 0)
        lax.while_loop(some, repair, clashes[k])
        return carry

    lax.fori_loop(0, recv_ref.shape[0] // peers, chunk, 0)
    head_rows(code_ref, recv_ref, w_in, w_mid, w_tile, head, sums)


def solve(head, dinv, corner, solved, solved_b):
    quarters = [head[q * HEAD : (q + 1) * HEAD, :] for q in range(HEAD // LANES)]
    rows = jnp.concatenate(quarters, axis=1)
    top = dot(dinv[0], rows[:BLOCK, :], lax.Precision.HIGHEST)
    top_b = top.astype(BF16)
    solved[:BLOCK, :] = top
    solved_b[:BLOCK, :] = top_b
    lost = dot(corner[:BLOCK, :], top_b[:LANES, :]) + dot(corner[BLOCK:, :], top_b[LANES:, :])
    rest = rows[BLOCK:, :] - lost
    low = dot(dinv[1], rest, lax.Precision.HIGHEST)
    solved[BLOCK:, :] = low
    solved_b[BLOCK:, :] = low.astype(BF16)


def update_kernel(
    first, panel_any, head, dinv, corner, slab, out, panel, result, solved_b, solved, in_sems, out_sems
):
    count = in_sems.shape[0]
    total = out.shape[0]
    rows = total // count

    def here(i):
        return pl.ds(pl.multiple_of(i * rows, rows), rows)

    def fetch(i):
        return pltpu.make_async_copy(panel_any.at[here(i), :], panel.at[here(i), :], in_sems.at[i])

    def give(i):
        return pltpu.make_async_copy(result.at[here(i), :], out.at[here(i), :], out_sems.at[i])

    for i in range(count):
        fetch(i).start()

    solve(head, dinv, corner, solved, solved_b)

    def step(i, carry):
        fetch(i).wait()
        for j in range(HEAD // (2 * LANES)):
            lost = dot(panel[here(i), :], solved_b[:, j * 2 * LANES : (j + 1) * 2 * LANES])
            for q in (2 * j, 2 * j + 1):
                start = pl.multiple_of(q * total + i * rows, rows)
                part = lost[:, (q - 2 * j) * LANES : (q - 2 * j + 1) * LANES]
                result[here(i), q * LANES : (q + 1) * LANES] = slab[pl.ds(start, rows), :] - part

        @pl.when(jnp.logical_and(first[0] == 1, i == 0))
        def _():
            result[:HEAD, :] = solved[...]

        give(i).start()
        return carry

    lax.fori_loop(0, count, step, 0)

    def finish(i, carry):
        give(i).wait()
        return carry

    lax.fori_loop(0, count, finish, 0)


def vmem():
    return pl.BlockSpec(memory_space=pltpu.VMEM)


def body(edge_feats, edge_rows, edge_cols, w_in, w_mid, w_out, cholesky_panel, diag_inverse):
    n_row = lax.axis_size("row")
    n_col = lax.axis_size("col")
    peers = n_row * n_col
    rows_dev = cholesky_panel.shape[0] * n_col
    slots = rows_dev // TILE
    panel = lax.all_gather(cholesky_panel, "col", axis=0, tiled=True)
    corner = cholesky_panel[BLOCK : 2 * BLOCK, :BLOCK]
    corner = jnp.concatenate([corner[:, :LANES], corner[:, LANES:]], axis=0).reshape(peers, 4, LANES)

    feats = edge_feats.reshape(peers, 16, LANES)
    row = (edge_rows % slots).reshape(peers, 16)
    col = (edge_cols % 32).reshape(peers, 16)
    place = jnp.concatenate([row // 32, row % 32, col], axis=1)
    both = jnp.concatenate(
        [place, jnp.tile(place[:n_col], (n_row, 1)), jnp.zeros((peers, 32), jnp.int32)], axis=1
    ).astype(BF16)
    payload = jnp.concatenate(
        [
            feats,
            jnp.tile(feats[:n_col], (n_row, 1, 1)),
            both[:, None, :],
            corner,
            jnp.zeros((peers, PAYLOAD - 37, LANES), BF16),
        ],
        axis=1,
    )
    recv = lax.all_to_all(payload, ("row", "col"), 0, 0, tiled=True)
    corner = jnp.broadcast_to(recv[:1, 33:37, :], (peers, 4, LANES))
    corner = lax.all_to_all(corner, ("row", "col"), 0, 0, tiled=True).reshape(2 * BLOCK, LANES)
    info = recv[:, 32, :96].astype(jnp.int32)
    own_row = info[:, 0:16] * 32 + info[:, 16:32]
    own_col = info[:, 32:48]
    window = own_col // GROUP * rows_dev + own_row * TILE
    dest = window.reshape(-1)
    later = iota((SET, SET), 1) > iota((SET, SET), 0)
    same = (window[:, :, None] == window[:, None, :]) & later
    bit = 1 << jnp.arange(16, dtype=jnp.int32)
    lost = jnp.sum(jnp.where(jnp.any(same, axis=2), bit, 0), axis=1)
    clashes = jnp.sum(jnp.where(lost.reshape(-1, CHUNK // SET) != 0, bit, 0), axis=1)
    lane = (own_col % GROUP).astype(F32)
    code = ((info[:, 48:64] * 32 + info[:, 64:80]) * 32 + info[:, 80:96]).reshape(-1, LANES)

    source = iota((256, 16 * LANES), 0)
    target = iota((256, 16 * LANES), 1)
    repeat = (source == target // LANES * TILE + target % TILE).astype(BF16)
    w_tile = dot(w_out, repeat).astype(BF16)

    slab, head = pl.pallas_call(
        assemble_kernel,
        out_shape=(
            pltpu.VMEM((rows_dev * HEAD // LANES, LANES), F32),
            pltpu.VMEM((HEAD * HEAD // LANES, LANES), F32),
        ),
        in_specs=[pl.BlockSpec(memory_space=pltpu.SMEM)] * 3 + [vmem()] * 6,
        out_specs=(vmem(), vmem()),
        scratch_shapes=[pltpu.VMEM((CHUNK * TILE, LANES), F32), pltpu.VMEM((LANES, 16 * LANES), F32)],
        compiler_params=pltpu.CompilerParams(vmem_limit_bytes=26 * MIB),
        cost_estimate=pl.CostEstimate(flops=15_000_000_000, bytes_accessed=24_000_000, transcendentals=0),
    )(dest, lost, clashes, code, recv, lane, w_in, w_mid, w_tile)

    first = (lax.axis_index("row") == 0).astype(jnp.int32).reshape(1)
    anywhere = pl.BlockSpec(memory_space=pl.ANY)
    return pl.pallas_call(
        update_kernel,
        out_shape=jax.ShapeDtypeStruct((rows_dev, HEAD), F32),
        in_specs=[pl.BlockSpec(memory_space=pltpu.SMEM), anywhere] + [vmem()] * 4,
        out_specs=anywhere,
        scratch_shapes=[
            pltpu.VMEM((rows_dev, HEAD), BF16),
            pltpu.VMEM((rows_dev, HEAD), F32),
            pltpu.VMEM((HEAD, HEAD), BF16),
            pltpu.VMEM((HEAD, HEAD), F32),
            pltpu.SemaphoreType.DMA((8,)),
            pltpu.SemaphoreType.DMA((8,)),
        ],
        compiler_params=pltpu.CompilerParams(vmem_limit_bytes=30 * MIB),
        cost_estimate=pl.CostEstimate(flops=4_300_000_000, bytes_accessed=42_000_000, transcendentals=0),
    )(
        first,
        pltpu.with_memory_space_constraint(panel, pltpu.HBM),
        pltpu.with_memory_space_constraint(head, pltpu.VMEM),
        diag_inverse,
        corner,
        pltpu.with_memory_space_constraint(slab, pltpu.VMEM),
    )


def solution(mesh):
    return jax.shard_map(
        body,
        mesh=mesh,
        in_specs=(
            P(("row", "col"), None),
            P(("row", "col")),
            P(("row", "col")),
            P(),
            P(),
            P(),
            P(("row", "col"), None),
            P(),
        ),
        out_specs=P("row", "col"),
        check_vma=False,
    )
```

time: 460 us -> 119 us (0.26); the launches traced: 454 us -> 118 us
  local copies, waits for them, and re-layouts: 262 us -> 22.8 us
  waiting for transfers between devices: 85.9 us -> 30.3 us
  matrix products: 45.2 us -> 2.11 us
  Pallas kernels: 0 us -> 30.6 us
  other arithmetic: 24.7 us -> 2.22 us
  starting transfers between devices: 21 us -> 16.2 us
    reshape x3 -> x4, local copies, waits for them, and re-layouts: 146 us -> 0.32 us  [the longest x1 0.08 us: body(): ((info[:, 48:64] * 32 + info[:, 64:80]) * 32 + info[:, 80:96]).reshape(-1...]
    transpose x1 -> x0, local copies, waits for them, and re-layouts: 88.5 us -> none  [body(): hamiltonian = assembled.reshape(row_slots, col_slots, TILE, TILE).transpo...]
    psum x2 -> x0, waiting for transfers between devices: 57.2 us -> none  [from_root(): return lax.psum(block, axis)]
    dot_general x6 -> x1, matrix products: 45.2 us -> 2.11 us  [dot(): return jnp.dot(a, b, precision=precision, preferred_element_type=F32)]
    pallas_call x0 -> x2, Pallas kernels: none -> 30.6 us  [the longest x1 21.5 us: body(): pl.pallas_call(assemble_kernel, out_shape=(pltpu.VMEM((rows_dev * HEAD //...]
    scatter-add x1 -> x0, other arithmetic: 18.7 us -> none  [body(): assembled = assembled.at[flat_place].add(received.reshape(-1, tile_size))]
    scatter-add x1 -> x0, local copies, waits for them, and re-layouts: 17.4 us -> none  [body(): assembled = assembled.at[flat_place].add(received.reshape(-1, tile_size))]
    unnamed x8 -> x16, local copies, waits for them, and re-layouts: 0.02 us -> 14.6 us
  transfers between devices with their start and end apart: 5 -> 3, of which waited for: 2 -> 2; matrix products, arithmetic and copies ran while one was open for 46% -> 11% of each run, Pallas kernels for 0% -> 18%
where the time goes in v1:
time: 119 us; the launch traced here: 118 us
  Pallas kernels  30.6 us (26%)
  waiting for transfers between devices  30.3 us (25%)
  local copies, waits for them, and re-layouts  22.8 us (19%)
  starting transfers between devices  16.2 us (14%)
  between operations  13.6 us (11%)
  other arithmetic  2.22 us (2%)
  matrix products  2.11 us (2%)
    all_to_all x1, waiting for transfers between devices, body(): recv = lax.all_to_all(payload, ('row', 'col'), 0, 0, tiled=True)  23.8 us
    pallas_call x1, Pallas kernels, body(): pl.pallas_call(assemble_kernel, out_shape=(pltpu.VMEM((rows_dev * HEAD //...  21.5 us
    unnamed x16, local copies, waits for them, and re-layouts  14.6 us
    all_to_all x1, starting transfers between devices, body(): recv = lax.all_to_all(payload, ('row', 'col'), 0, 0, tiled=True)  11.1 us
    pallas_call x1, Pallas kernels, body(): pl.pallas_call(update_kernel, out_shape=jax.ShapeDtypeStruct((rows_dev, H...  9.11 us
    all_gather x1, waiting for transfers between devices, body(): panel = lax.all_gather(cholesky_panel, 'col', axis=0, tiled=True)  5.78 us
    all_to_all x1, starting transfers between devices, body(): lax.all_to_all(corner, ('row', 'col'), 0, 0, tiled=True)  5.05 us
    concatenate x1, local copies, waits for them, and re-layouts, body(): jnp.concatenate([feats, jnp.tile(feats[:n_col], (n_row, 1, 1)), both[:, N...  3.9 us
  transfers between devices with their start and end apart: 3, of which 2 were waited for; matrix products, arithmetic and copies ran while one was open for 11% of the time, Pallas kernels for 18%

profile of v1, /device:TPU:0, one launch (start us, length us, event | category | flops | bytes accessed | tf_op | source)
XLA Modules:
  0.0 117.9 jit_solution(6613400378268380158)
XLA Ops:
  6.5 0.7 all-gather.2.cloned.1.call-update
  7.3 0.7 add_select_fusion.4
  8.1 0.7 add_select_fusion.5
  8.8 0.1 concatenate.37
  8.9 0.8 slice.40
  10.2 1.0 concatenate.34
  11.2 0.9 fusion.30
  12.2 3.9 %concatenate.36 = bf16[128,40,128]{2,1,0:T(8,128)(2,1)} concatenate(bf16[128,16,128]{2,1,0:T(8,128)(2,1)S(1)} %bitcast.23, bf16[128,16,128]{2,1,0:T(8,128)(2,1)S(1)} %bitcast.22, bf16[128,1,128]{2,1,0:T(2,128)(2,1)S(1)} %concatenate.34, bf16[128,4,128]{2,1,0:T(4,128)(2,1)S(1)} %bitcast.24, bf16[128,3,128]{2,1,0:T(4,128)(2,1)S(1)} %broadcast_in_dim.30), dimensions={1} | concatenate | bytes 2621440 | tf_op jit(solution)/shard_map/concatenate | solution.py:245
  16.1 11.1 %all-to-all-start = ((bf16[128,40,128]{2,1,0:T(8,128)(2,1)}), bf16[128,40,128]{2,1,0:T(8,128)(2,1)S(1)}, u32[]{:S(2)}, u32[]{:S(2)}) async-start(bf16[128,40,128]{2,1,0:T(8,128)(2,1)} %concatenate.36), calls=%async_computation | async-start | bytes 2621440 | tf_op jit(solution)/shard_map/all_to_all | solution.py:255
  27.4 2.1 %fusion.w_tile = bf16[512,2048]{1,0:T(8,128)(2,1)} fusion(bf16[512,256]{1,0:T(8,128)(2,1)S(1)} %copy-done, s32[2048]{0:T(1024)S(1)} %get-tuple-element.23, s32[2048]{0:T(1024)S(1)} %get-tuple-element.25, s32[2048]{0:T(1024)S(1)} %get-tuple-element.24, s32[2048]{0:T(1024)S(1)} %get-tuple-element.26, pred[2048]{0:T(1024)(128)(4,1)S(1)} %get-tuple-element.28, ...), kind=kOutput, calls=%fused_computation.1 | convolution fusion | flops 540540928 | bytes 2396160 | tf_op jit(solution)/shard_map/dot_general | solution.py:23
  29.5 23.8 %all-to-all-done.recv_ref = bf16[128,40,128]{2,1,0:T(8,128)(2,1)S(1)} async-done(((bf16[128,40,128]{2,1,0:T(8,128)(2,1)}), bf16[128,40,128]{2,1,0:T(8,128)(2,1)S(1)}, u32[]{:S(2)}, u32[]{:S(2)}) %all-to-all-start) | async-done | bytes 1310752 | tf_op jit(solution)/shard_map/all_to_all | solution.py:255
  53.4 0.1 fusion.10
  53.5 0.2 slice_add_fusion
  53.9 0.1 and_reduce_fusion
  54.2 0.7 broadcast_in_dim.34
  54.9 5.1 %all-to-all-start.1 = ((bf16[128,4,128]{2,1,0:T(4,128)(2,1)}), bf16[128,4,128]{2,1,0:T(4,128)(2,1)S(1)}, u32[]{:S(2)}, u32[]{:S(2)}) async-start(bf16[128,4,128]{2,1,0:T(4,128)(2,1)} %broadcast_in_dim.34), calls=%async_computation.1 | async-start | bytes 262144 | tf_op jit(solution)/shard_map/all_to_all | solution.py:257
  60.0 0.1 select_reduce_fusion.1.clashes
  60.1 1.0 copy-done.4
  61.1 1.6 %copy-done.6 = bf16[512,2048]{1,0:T(8,128)(2,1)S(1)} copy-done((bf16[512,2048]{1,0:T(8,128)(2,1)S(1)}, bf16[512,2048]{1,0:T(8,128)(2,1)}, u32[]{:S(2)}) %copy-start.6) | copy-done | bytes 2097176
  62.7 21.5 %shard_map.82 = (f32[32768,128]{1,0:T(8,128)S(1)}, f32[2048,128]{1,0:T(8,128)S(1)}) custom-call(s32[2048]{0:T(1024)S(1)} %reshape.124.dest, s32[128]{0:T(128)S(1)} %select_reduce_fusion.lost, s32[8]{0:T(128)S(1)} %select_reduce_fusion.1.clashes, s32[16,128]{1,0:T(8,128)S(1)} %reshape.125.code_ref, bf16[128,40,128]{2,1,0:T(8,128)(2,1)S(1)} %all-to-all-done.recv_ref, ...), custom_call_target="tpu_custom_call" | custom-call | flops 15000000512 | bytes 24000000 | tf_op jit(solution)/shard_map/pallas_call | solution.py:276
  84.2 6.2 %copy-done.1 = f32[32768,128]{1,0:T(8,128)} copy-done((f32[32768,128]{1,0:T(8,128)}, f32[32768,128]{1,0:T(8,128)S(1)}, u32[]{:S(2)}) %copy-start.1) | copy-done | bytes 16777240
  90.4 5.8 %all-gather.2.cloned.1.call-done.panel_any = bf16[8192,512]{1,0:T(8,128)(2,1)} async-done(((bf16[512,512]{1,0:T(8,128)(2,1)}), bf16[8192,512]{1,0:T(8,128)(2,1)}) %all-gather.2.cloned.1.call-update) | async-done | bytes 8388624 | tf_op jit(solution)/shard_map/all_gather | solution.py:234
  96.1 5.8 %copy-done.2 = f32[32768,128]{1,0:T(8,128)S(1)} copy-done((f32[32768,128]{1,0:T(8,128)S(1)}, f32[32768,128]{1,0:T(8,128)}, u32[]{:S(2)}) %copy-start.2) | copy-done | bytes 16777240
  101.9 9.1 %shard_map.83 = f32[8192,512]{1,0:T(8,128)} custom-call(s32[1]{0:T(128)} %bitcast.first, bf16[8192,512]{1,0:T(8,128)(2,1)} %all-gather.2.cloned.1.call-done.panel_any, f32[2048,128]{1,0:T(8,128)S(1)} %get-tuple-element.7.head, f32[2,256,256]{2,1,0:T(8,128)S(1)} %copy-done.3, bf16[512,128]{1,0:T(8,128)(2,1)S(1)} %bitcast.21, f32[32768,128]{1,0:T(8,128)S(1)} %copy-done.2), custom_call_target="tpu_custom_call" | custom-call | flops 4300000256 | bytes 42000000 | tf_op jit(solution)/shard_map/pallas_call | solution.py:291
  (40 shorter events, 1.2 us)
Async XLA Ops:
  6.5 20.8 %copy-start = (bf16[512,256]{1,0:T(8,128)(2,1)S(1)}, bf16[512,256]{1,0:T(8,128)(2,1)}, u32[]{:S(2)}) copy-start(bf16[512,256]{1,0:T(8,128)(2,1)} %param.13) | copy-start | bytes 786436
  6.5 5.7 %copy-start.7 = (bf16[2048,128]{1,0:T(8,128)(2,1)S(1)}, bf16[2048,128]{1,0:T(8,128)(2,1)}, u32[]{:S(2)}) copy-start(bf16[2048,128]{1,0:T(8,128)(2,1)} %param.8) | copy-start | bytes 1572868
  6.5 89.6 %all-gather.2.cloned.1.call-start = ((), (), s32[]{:S(2)}) async-start(), calls=%async_computation.2 | async-start | bytes 8912896 | tf_op jit(solution)/shard_map/all_gather | solution.py:234
  16.1 37.2 %all-to-all-start = ((bf16[128,40,128]{2,1,0:T(8,128)(2,1)}), bf16[128,40,128]{2,1,0:T(8,128)(2,1)S(1)}, u32[]{:S(2)}, u32[]{:S(2)}) async-start(bf16[128,40,128]{2,1,0:T(8,128)(2,1)} %concatenate.36), calls=%async_computation | async-start | bytes 2621440 | tf_op jit(solution)/shard_map/all_to_all | solution.py:255
  27.4 32.7 %copy-start.5 = (bf16[128,512]{1,0:T(8,128)(2,1)S(1)}, bf16[128,512]{1,0:T(8,128)(2,1)}, u32[]{:S(2)}) copy-start(bf16[128,512]{1,0:T(8,128)(2,1)} %w_in.1) | copy-start | bytes 393220
  54.9 35.5 %all-to-all-start.1 = ((bf16[128,4,128]{2,1,0:T(4,128)(2,1)}), bf16[128,4,128]{2,1,0:T(4,128)(2,1)S(1)}, u32[]{:S(2)}, u32[]{:S(2)}) async-start(bf16[128,4,128]{2,1,0:T(4,128)(2,1)} %broadcast_in_dim.34), calls=%async_computation.1 | async-start | bytes 262144 | tf_op jit(solution)/shard_map/all_to_all | solution.py:257
  60.1 1.0 copy-start.4
  61.1 1.6 %copy-start.6 = (bf16[512,2048]{1,0:T(8,128)(2,1)S(1)}, bf16[512,2048]{1,0:T(8,128)(2,1)}, u32[]{:S(2)}) copy-start(bf16[512,2048]{1,0:T(8,128)(2,1)} %fusion.w_tile) | copy-start | bytes 6291460
  62.7 33.4 %copy-start.3 = (f32[2,256,256]{2,1,0:T(8,128)S(1)}, f32[2,256,256]{2,1,0:T(8,128)}, u32[]{:S(2)}) copy-start(f32[2,256,256]{2,1,0:T(8,128)} %dinv.1) | copy-start | bytes 1572868
  84.2 6.2 %copy-start.1 = (f32[32768,128]{1,0:T(8,128)}, f32[32768,128]{1,0:T(8,128)S(1)}, u32[]{:S(2)}) copy-start(f32[32768,128]{1,0:T(8,128)S(1)} %get-tuple-element.8.slab) | copy-start | bytes 50331652
  96.1 5.8 %copy-start.2 = (f32[32768,128]{1,0:T(8,128)S(1)}, f32[32768,128]{1,0:T(8,128)}, u32[]{:S(2)}) copy-start(f32[32768,128]{1,0:T(8,128)} %copy-done.1) | copy-start | bytes 50331652
Sparse Core Ops, SparseCore 0:
  9.5 86.5 all-gather.1

commit v2 on v1

v2 whole, which is shorter than its diff:
```python
import functools

import jax
import jax.numpy as jnp
from jax import lax
from jax.experimental import pallas as pl
from jax.experimental.pallas import tpu as pltpu
from jax.sharding import PartitionSpec as P

TILE = 16
BLOCK = 256
HEAD = 512
LANES = 128
GROUP = 8
CHUNK = 256
HIDDEN = 512
SET = 16
PASS = 256
PAYLOAD = 40
MIB = 1024 * 1024
F32 = jnp.float32
BF16 = jnp.bfloat16


def dot(a, b, precision=None):
    return jnp.dot(a, b, precision=precision, preferred_element_type=F32)


def dot_t(a, b):
    return lax.dot_general(a, b, (((1,), (1,)), ((), ())), preferred_element_type=F32)


def silu(v):
    half = 0.5 * v
    return half + half * jnp.tanh(half)


def hidden(feats, w_in, w_mid):
    one = silu(dot(feats, w_in)).astype(BF16)
    return silu(dot(one, w_mid)).astype(BF16)


def iota(shape, dim):
    return lax.broadcasted_iota(jnp.int32, shape, dim)


def head_rows(code_ref, recv_ref, w_in, w_mid, w_tile, head, sums):
    code = code_ref[...]
    slot = code // 32
    column = code % 32
    groups = code.shape[0]
    keep = slot < HEAD // TILE
    ones = jnp.where(keep, 1.0, 0.0).astype(F32)
    upto = jnp.where(iota((LANES, LANES), 0) <= iota((LANES, LANES), 1), 1.0, 0.0).astype(BF16)
    before = jnp.where(iota((groups, groups), 1) < iota((groups, groups), 0), 1.0, 0.0).astype(BF16)
    totals = jnp.broadcast_to(jnp.sum(ones, axis=1, keepdims=True), ones.shape)
    place = dot(ones.astype(BF16), upto) + dot(before, totals.astype(BF16)) - 1.0
    place = jnp.where(keep, place, -1.0)
    count = jnp.sum(ones).astype(jnp.int32)
    slot_f = slot.astype(F32)
    column_f = column.astype(F32)
    sums[...] = jnp.zeros_like(sums)

    def one_pass(step, carry):
        wanted = (iota((PASS, LANES), 0) + step * PASS).astype(F32)
        feats = jnp.zeros((PASS, LANES), F32)
        by_row = jnp.zeros((16, PASS), F32)
        by_col = jnp.zeros((PASS, 16), F32)
        which = iota((16, LANES), 0)
        for g in range(groups):
            pick = jnp.where(place[g : g + 1, :] == wanted, 1.0, 0.0).astype(BF16)
            block = recv_ref[g * 8 : (g + 1) * 8, 16:32, :].reshape(LANES, LANES)
            feats += dot(pick, block)
            where_to = jnp.where(
                which == 0, slot_f[g : g + 1, :], jnp.where(which == 1, column_f[g : g + 1, :], 0.0)
            ).astype(BF16)
            by_row += dot_t(where_to, pick)
            by_col += dot_t(pick, where_to)
        two = hidden(feats.astype(BF16), w_in[...], w_mid[...])
        col_c = by_col[:, 1:2].astype(jnp.int32)
        mask = iota((PASS, 2 * LANES), 1) % LANES // TILE == col_c % GROUP
        row_c = by_row[1:2, :].astype(jnp.int32)
        key = row_c // GROUP * (HEAD // TILE) + by_row[0:1, :].astype(jnp.int32)
        spread = jnp.where(iota((LANES, PASS), 0) == key, 1.0, 0.0).astype(F32)
        for j in range(TILE // 2):
            lanes = slice(j * 2 * LANES, (j + 1) * 2 * LANES)
            values = jnp.where(mask, dot(two, w_tile[:, lanes]), 0.0)
            sums[:, lanes] += dot(spread, values, lax.Precision.HIGHEST)
        return carry

    lax.fori_loop(0, (count + PASS - 1) // PASS, one_pass, 0)
    per = HEAD // TILE
    for a in range(TILE):
        for q in range(HEAD // LANES):
            head[pl.ds(q * HEAD + a, per, stride=TILE), :] = sums[
                q * per : (q + 1) * per, a * LANES : (a + 1) * LANES
            ]


def solve(head, dinv, corner, solved, solved_b):
    quarters = [head[q * HEAD : (q + 1) * HEAD, :] for q in range(HEAD // LANES)]
    rows = jnp.concatenate(quarters, axis=1)
    top = dot(dinv[0], rows[:BLOCK, :], lax.Precision.HIGHEST)
    top_b = top.astype(BF16)
    solved[:BLOCK, :] = top
    solved_b[:BLOCK, :] = top_b
    lost = dot(corner[:BLOCK, :], top_b[:LANES, :]) + dot(corner[BLOCK:, :], top_b[LANES:, :])
    rest = rows[BLOCK:, :] - lost
    low = dot(dinv[1], rest, lax.Precision.HIGHEST)
    solved[BLOCK:, :] = low
    solved_b[BLOCK:, :] = low.astype(BF16)


def some(bits):
    return bits != 0


def low_bit(bits):
    low = bits & -bits
    place = 0
    for width, mask in ((8, 0xFF00), (4, 0xF0F0), (2, 0xCCCC), (1, 0xAAAA)):
        place = place + jnp.where((low & mask) != 0, width, 0)
    return place


def hidden_kernel(code, recv, w_in, w_mid, w_tile, two, head, sums):
    def chunk(k, carry):
        peers = HIDDEN // SET
        feats = recv[pl.ds(pl.multiple_of(k * peers, peers), peers), 0:16, :].reshape(HIDDEN, LANES)
        two[pl.ds(pl.multiple_of(k * HIDDEN, HIDDEN), HIDDEN), :] = hidden(feats, w_in[...], w_mid[...])
        return carry

    head_rows(code, recv, w_in, w_mid, w_tile, head, sums)
    lax.fori_loop(0, two.shape[0] // HIDDEN, chunk, 0)


def assemble(dest, lost, clashes, two, lane_ref, w_tile, slab, tiles, early):
    peers = CHUNK // SET

    def clear(i, carry):
        slab[pl.ds(pl.multiple_of(i * 512, 512), 512), :] = jnp.zeros((512, LANES), F32)
        return carry

    lax.fori_loop(0, slab.shape[0] // 512, clear, 0)
    for copy in early:
        copy.wait()

    def chunk(k, carry):
        start = pl.multiple_of(k * peers, peers)
        rows = two[pl.ds(pl.multiple_of(k * CHUNK, CHUNK), CHUNK), :]
        lane = lane_ref[pl.ds(start, peers), :]
        lane = jnp.broadcast_to(lane[:, None, :], (peers, 16, 16)).reshape(CHUNK, 16)
        own = iota((CHUNK, 16), 0) % 16 == iota((CHUNK, 16), 1)
        lane = jnp.sum(jnp.where(own, lane, 0.0), axis=1, keepdims=True).astype(jnp.int32)
        mask = iota((CHUNK, LANES), 1) // TILE == lane
        for j in range(TILE // 2):
            pair = dot(rows, w_tile[:, j * 2 * LANES : (j + 1) * 2 * LANES])
            for i in range(2):
                tiles[pl.ds(2 * j + i, CHUNK, stride=TILE), :] = jnp.where(
                    mask, pair[:, i * LANES : (i + 1) * LANES], 0.0
                )

        def load(e):
            return tiles[pl.ds(pl.multiple_of(e * TILE, TILE), TILE), :]

        def place(i, inner):
            at = [pl.multiple_of(dest[k * CHUNK + i * SET + e], TILE) for e in range(SET)]
            sums = [slab[pl.ds(at[e], TILE), :] + load(i * SET + e) for e in range(SET)]
            for e in range(SET):
                slab[pl.ds(at[e], TILE), :] = sums[e]
            return inner

        def repair(bits):
            peer = low_bit(bits)

            def one(left):
                e = peer * SET + low_bit(left)
                at = pl.multiple_of(dest[k * CHUNK + e], TILE)
                slab[pl.ds(at, TILE), :] += load(e)
                return left & (left - 1)

            lax.while_loop(some, one, lost[k * peers + peer])
            return bits & (bits - 1)

        lax.fori_loop(0, CHUNK // SET, place, 0)
        lax.while_loop(some, repair, clashes[k])
        return carry

    lax.fori_loop(0, two.shape[0] // CHUNK, chunk, 0)


def final_kernel(count, *refs):
    place, dest, lost, clashes, two, lane, w_tile, head, dinv, corner = refs[:10]
    pieces = refs[10 : 10 + count]
    out, solved_b = refs[10 + count : 12 + count]
    slab, tiles, solved, panel, result, two_v, tile_v, in_sems, out_sems, sems = refs[12 + count :]
    total = out.shape[0]
    blocks = out_sems.shape[0]
    rows = total // blocks
    copies = [pltpu.make_async_copy(piece, panel.at[i], in_sems.at[i]) for i, piece in enumerate(pieces)]
    early = [pltpu.make_async_copy(two, two_v, sems.at[0]), pltpu.make_async_copy(w_tile, tile_v, sems.at[1])]
    for copy in early + copies:
        copy.start()
    solve(head, dinv, corner, solved, solved_b)
    assemble(dest, lost, clashes, two_v, lane, tile_v, slab, tiles, early)
    for copy in copies:
        copy.wait()

    def block(i):
        return pl.ds(pl.multiple_of(i * rows, rows), rows)

    def give(i):
        return pltpu.make_async_copy(result.at[block(i), :], out.at[block(place[i]), :], out_sems.at[i])

    def part(i, q):
        return slab[pl.ds(pl.multiple_of(q * total + place[i] * rows, rows), rows), :]

    def leave(i):
        @pl.when(jnp.logical_and(place[blocks] == 1, place[i] == 0))
        def _():
            result[block(i), :] = solved[...]

        give(i).start()

    def step(i, carry):
        for j in range(HEAD // (2 * LANES)):
            less = dot(panel[i], solved_b[:, j * 2 * LANES : (j + 1) * 2 * LANES])
            for q in (2 * j, 2 * j + 1):
                lanes = slice((q - 2 * j) * LANES, (q - 2 * j + 1) * LANES)
                result[block(i), q * LANES : (q + 1) * LANES] = part(i, q) - less[:, lanes]
        leave(i)
        return carry

    def plain(i, carry):
        for q in range(HEAD // LANES):
            result[block(i), q * LANES : (q + 1) * LANES] = part(i, q)
        leave(i)
        return carry

    lax.fori_loop(count, blocks, plain, 0)
    lax.fori_loop(0, count, step, 0)

    def finish(i, carry):
        give(i).wait()
        return carry

    lax.fori_loop(0, blocks, finish, 0)


def last_kernel(first, *refs):
    place, solved_b, before = refs[:3]
    count = place.shape[0] - 1 - first
    pieces = refs[3 : 3 + count]
    out, panel, result, in_sems, take_sems, out_sems = refs[3 + count :]
    rows = pieces[0].shape[0]

    def block(i):
        return pl.ds(pl.multiple_of(place[first + i] * rows, rows), rows)

    fetches = [pltpu.make_async_copy(pieces[i], panel.at[i], in_sems.at[i]) for i in range(count)]
    takes = [pltpu.make_async_copy(before.at[block(i), :], result.at[i], take_sems.at[i]) for i in range(count)]
    gives = [pltpu.make_async_copy(result.at[i], out.at[block(i), :], out_sems.at[i]) for i in range(count)]
    for copy in fetches + takes:
        copy.start()
    for i in range(count):
        fetches[i].wait()
        takes[i].wait()

        @pl.when(jnp.logical_not(jnp.logical_and(place[first + count] == 1, place[first + i] == 0)))
        def _():
            for j in range(HEAD // (2 * LANES)):
                lanes = slice(j * 2 * LANES, (j + 1) * 2 * LANES)
                result[i, :, lanes] -= dot(panel[i], solved_b[:, lanes])

        gives[i].start()
    for copy in gives:
        copy.wait()


def vmem():
    return pl.BlockSpec(memory_space=pltpu.VMEM)


def payload_kernel(feats, rows, cols, corner, out):
    peers = feats.shape[0]
    n_col = 16
    groups, per = rows.shape[0], peers // rows.shape[0]
    code = (rows[...] & 511) * 32 + (cols[...] & 31)
    high, low = (code >> 7).astype(F32), (code & 127).astype(F32)
    line = iota((8, LANES), 0)
    out[:, 0:16, :] = feats[...]
    for i in range(peers // n_col):
        out[i * n_col : (i + 1) * n_col, 16:32, :] = feats[:n_col, :, :]
    for g in range(groups):
        h = g % (n_col // per)
        block = jnp.where(line == 0, high[g : g + 1, :], low[g : g + 1, :])
        block = jnp.where(line == 2, high[h : h + 1, :], jnp.where(line == 3, low[h : h + 1, :], block))
        block = jnp.broadcast_to(block[None], (per, 8, LANES))
        slices = corner[g * per : (g + 1) * per, :, :].astype(F32)
        out[g * per : (g + 1) * per, 32:40, :] = jnp.where(line[None] < 4, block, slices).astype(BF16)


def along_x(value, by):
    return lax.ppermute(value, "col", [(z * 4 + x, z * 4 + (x + by) % 4) for z in range(4) for x in range(4)])


def along_z(value, by):
    return lax.ppermute(value, "col", [(z * 4 + x, (z + by) % 4 * 4 + x) for z in range(4) for x in range(4)])


def start_gather(own):
    got = {"own": own}
    got["left"], got["right"] = along_x(own, 1), along_x(own, -1)
    got["down"], got["up"] = along_z(own, 1), along_z(own, -1)
    return got


def together(got, *others):
    values = lax.optimization_barrier((*got.values(), *others))
    return dict(zip(got, values[: len(got)], strict=True)), *values[len(got) :]


def second_gather(near):
    got = {(0, 0): near["own"], (-1, 0): near["left"], (1, 0): near["right"], (0, -1): near["down"], (0, 1): near["up"]}
    got[1, 1] = along_x(got[0, 1], -1)
    got[1, -1] = along_z(got[1, 0], 1)
    got[-1, 1] = along_z(got[-1, 0], -1)
    got[-1, -1] = along_x(got[0, -1], 1)
    return got


def third_gather(got):
    got[2, 1] = along_x(got[1, 1], -1)
    got[-1, 2] = along_z(got[-1, 1], -1)
    got[2, 0] = along_x(got[-1, 0], 1)
    got[0, 2] = along_z(got[0, -1], 1)
    return got


def fourth_gather(got):
    got[2, -1] = along_x(got[1, -1], -1)
    got[1, 2] = along_z(got[1, 1], -1)
    got[2, 2] = along_x(got[-1, 2], 1)
    return got


def body(edge_feats, edge_rows, edge_cols, w_in, w_mid, w_out, cholesky_panel, diag_inverse):
    n_row = lax.axis_size("row")
    n_col = lax.axis_size("col")
    peers = n_row * n_col
    rows_dev = cholesky_panel.shape[0] * n_col
    slots = rows_dev // TILE
    got = start_gather(cholesky_panel)
    corner = cholesky_panel[BLOCK : 2 * BLOCK, :BLOCK]
    corner = jnp.concatenate([corner[:, :LANES], corner[:, LANES:]], axis=0).reshape(peers, 4, LANES)
    corner = jnp.pad(corner, ((0, 0), (4, 0), (0, 0)))

    feats = edge_feats.reshape(peers, 16, LANES)
    payload = pl.pallas_call(
        payload_kernel,
        out_shape=jax.ShapeDtypeStruct((peers, PAYLOAD, LANES), BF16),
        in_specs=[vmem()] * 4,
        out_specs=vmem(),
        compiler_params=pltpu.CompilerParams(vmem_limit_bytes=16 * MIB),
    )(feats, edge_rows.reshape(16, LANES), edge_cols.reshape(16, LANES), corner)
    payload, got = lax.optimization_barrier((payload, got))
    recv = lax.all_to_all(payload, ("row", "col"), 0, 0, tiled=True)
    corner = jnp.broadcast_to(recv[:1, 36:40, :], (peers, 4, LANES))
    corner = lax.all_to_all(corner, ("row", "col"), 0, 0, tiled=True).reshape(2 * BLOCK, LANES)
    own_lane = lax.axis_index("col") % GROUP * 16
    info = lax.dynamic_slice(recv, (0, 32, own_lane), (peers, 4, 16)).astype(jnp.int32)
    own = info[:, 0, :] * 128 + info[:, 1, :]
    own_row, own_col = own // 32, own % 32
    window = own_col // GROUP * rows_dev + own_row * TILE
    dest = window.reshape(-1)
    code = (info[:, 2, :] * 128 + info[:, 3, :]).reshape(-1, LANES)
    later = iota((SET, SET), 1) > iota((SET, SET), 0)
    same = (window[:, :, None] == window[:, None, :]) & later
    bit = 1 << jnp.arange(16, dtype=jnp.int32)
    lost = jnp.sum(jnp.where(jnp.any(same, axis=2), bit, 0), axis=1)
    clashes = jnp.sum(jnp.where(lost.reshape(-1, CHUNK // SET) != 0, bit, 0), axis=1)
    lane = (own_col % GROUP).astype(F32)

    source = iota((256, 16 * LANES), 0)
    target = iota((256, 16 * LANES), 1)
    repeat = (source == target // LANES * TILE + target % TILE).astype(BF16)
    w_tile = dot(w_out, repeat).astype(BF16)

    anywhere = pl.BlockSpec(memory_space=pl.ANY)
    smem = pl.BlockSpec(memory_space=pltpu.SMEM)
    got, recv = together(second_gather(got), recv)
    got = third_gather(got)
    two, head = pl.pallas_call(
        hidden_kernel,
        out_shape=(
            jax.ShapeDtypeStruct((16 * peers, w_mid.shape[1]), BF16),
            jax.ShapeDtypeStruct((HEAD * HEAD // LANES, LANES), F32),
        ),
        in_specs=[vmem()] * 5,
        out_specs=(vmem(), vmem()),
        scratch_shapes=[pltpu.VMEM((LANES, 16 * LANES), F32)],
        compiler_params=pltpu.CompilerParams(vmem_limit_bytes=20 * MIB),
        cost_estimate=pl.CostEstimate(flops=10_000_000_000, bytes_accessed=8_000_000, transcendentals=0),
    )(code, recv, w_in, w_mid, w_tile)
    got, two, head = together(got, two, head)
    ready = len(got)
    got = fourth_gather(got)
    me = lax.axis_index("col")
    x, z = me % 4, me // 4
    place = [(z + dz) % 4 * 4 + (x + dx) % 4 for dx, dz in got]
    place = jnp.stack(place + [(lax.axis_index("row") == 0).astype(jnp.int32)]).astype(jnp.int32)
    count = len(got)
    pieces = list(got.values())
    held = [pltpu.with_memory_space_constraint(value, pltpu.HBM) for value in pieces[:ready]]
    part, solved_b = pl.pallas_call(
        functools.partial(final_kernel, ready),
        out_shape=(
            jax.ShapeDtypeStruct((rows_dev, HEAD), F32),
            jax.ShapeDtypeStruct((HEAD, HEAD), BF16),
        ),
        in_specs=[smem] * 4 + [anywhere, vmem(), anywhere] + [vmem()] * 3 + [anywhere] * ready,
        out_specs=(anywhere, vmem()),
        scratch_shapes=[
            pltpu.VMEM((rows_dev * HEAD // LANES, LANES), F32),
            pltpu.VMEM((CHUNK * TILE, LANES), F32),
            pltpu.VMEM((HEAD, HEAD), F32),
            pltpu.VMEM((ready, *cholesky_panel.shape), BF16),
            pltpu.VMEM((rows_dev, HEAD), F32),
            pltpu.VMEM(two.shape, BF16),
            pltpu.VMEM(w_tile.shape, BF16),
            pltpu.SemaphoreType.DMA((ready,)),
            pltpu.SemaphoreType.DMA((count,)),
            pltpu.SemaphoreType.DMA((2,)),
        ],
        compiler_params=pltpu.CompilerParams(vmem_limit_bytes=56 * MIB),
        cost_estimate=pl.CostEstimate(flops=15_000_000_000, bytes_accessed=30_000_000, transcendentals=0),
    )(place, dest, lost, clashes, two, lane, w_tile, head, diag_inverse, corner, *held)
    left = count - ready
    return pl.pallas_call(
        functools.partial(last_kernel, ready),
        out_shape=jax.ShapeDtypeStruct((rows_dev, HEAD), F32),
        in_specs=[smem, vmem()] + [anywhere] * (1 + left),
        out_specs=anywhere,
        scratch_shapes=[
            pltpu.VMEM((left, *cholesky_panel.shape), BF16),
            pltpu.VMEM((left, cholesky_panel.shape[0], HEAD), F32),
            pltpu.SemaphoreType.DMA((left,)),
            pltpu.SemaphoreType.DMA((left,)),
            pltpu.SemaphoreType.DMA((left,)),
        ],
        input_output_aliases={2: 0},
        compiler_params=pltpu.CompilerParams(vmem_limit_bytes=16 * MIB),
        cost_estimate=pl.CostEstimate(flops=800_000_000, bytes_accessed=8_000_000, transcendentals=0),
    )(place, solved_b, part, *pieces[ready:])


def solution(mesh):
    return jax.shard_map(
        body,
        mesh=mesh,
        in_specs=(
            P(("row", "col"), None),
            P(("row", "col")),
            P(("row", "col")),
            P(),
            P(),
            P(),
            P(("row", "col"), None),
            P(),
        ),
        out_specs=P("row", "col"),
        check_vma=False,
    )
```

time: 119 us -> 114 us (0.958)
  starting transfers between devices: 16.2 us -> 38 us
  between operations: 13.6 us -> 0.58 us
  local copies, waits for them, and re-layouts: 22.8 us -> 10.8 us
  waiting for transfers between devices: 30.3 us -> 20.7 us
  Pallas kernels: 30.6 us -> 38.6 us
    ppermute x0 -> x15, starting transfers between devices: none -> 24.1 us  [the longest x7 12.1 us: along_z(): lax.ppermute(value, 'col', [(z * 4 + x, (z + by) % 4 * 4 + x) for z in ra...]
    all_to_all x1, waiting for transfers between devices: 23.8 us -> 12.7 us  [body(): recv = lax.all_to_all(payload, ('row', 'col'), 0, 0, tiled=True)]
    pallas_call x2 -> x4, Pallas kernels: 30.6 us -> 38.6 us  [the longest x1 26.2 us: body(): pl.pallas_call(functools.partial(final_kernel, ready), out_shape=(jax.Sha...]
    ppermute x0 -> x15, waiting for transfers between devices: none -> 8.04 us  [the longest x7 5.08 us: along_z(): lax.ppermute(value, 'col', [(z * 4 + x, (z + by) % 4 * 4 + x) for z in ra...]
    unnamed x16 -> x28, local copies, waits for them, and re-layouts: 14.6 us -> 8.05 us
    all_gather x1 -> x0, waiting for transfers between devices: 5.78 us -> none  [body(): panel = lax.all_gather(cholesky_panel, 'col', axis=0, tiled=True)]
    concatenate x6 -> x0, local copies, waits for them, and re-layouts: 5.17 us -> none  [the longest x1 3.9 us: body(): jnp.concatenate([feats, jnp.tile(feats[:n_col], (n_row, 1, 1)), both[:, N...]
    all_to_all x1, starting transfers between devices: 11.1 us -> 9.22 us  [body(): recv = lax.all_to_all(payload, ('row', 'col'), 0, 0, tiled=True)]
  transfers between devices with their start and end apart: 3 -> 17, of which waited for: 2 -> 5; matrix products, arithmetic and copies ran while one was open for 11% -> 7% of each run, Pallas kernels for 18% -> 30%
where the time goes in v2:
time: 114 us; the launch traced here: 113 us
  Pallas kernels  38.6 us (34%)
  starting transfers between devices  38 us (33%)
  waiting for transfers between devices  20.7 us (18%)
  local copies, waits for them, and re-layouts  10.8 us (9%)
  other arithmetic  2.48 us (2%)
  matrix products  2.14 us (2%)
    pallas_call x1, Pallas kernels, body(): pl.pallas_call(functools.partial(final_kernel, ready), out_shape=(jax.Sha...  26.2 us
    all_to_all x1, waiting for transfers between devices, body(): recv = lax.all_to_all(payload, ('row', 'col'), 0, 0, tiled=True)  12.7 us
    ppermute x7, starting transfers between devices, along_z(): lax.ppermute(value, 'col', [(z * 4 + x, (z + by) % 4 * 4 + x) for z in ra...  12.1 us
    ppermute x8, starting transfers between devices, along_x(): lax.ppermute(value, 'col', [(z * 4 + x, z * 4 + (x + by) % 4) for z in ra...  12 us
    all_to_all x1, starting transfers between devices, body(): recv = lax.all_to_all(payload, ('row', 'col'), 0, 0, tiled=True)  9.22 us
    unnamed x28, local copies, waits for them, and re-layouts  8.05 us
    pallas_call x1, Pallas kernels, body(): pl.pallas_call(hidden_kernel, out_shape=(jax.ShapeDtypeStruct((16 * peers...  6.95 us
    ppermute x7, waiting for transfers between devices, along_z(): lax.ppermute(value, 'col', [(z * 4 + x, (z + by) % 4 * 4 + x) for z in ra...  5.08 us
  transfers between devices with their start and end apart: 17, of which 5 were waited for; matrix products, arithmetic and copies ran while one was open for 7% of the time, Pallas kernels for 30%

profile of v2, /device:TPU:0, one launch (start us, length us, event | category | flops | bytes accessed | tf_op | source)
XLA Modules:
  0.0 113.4 jit_solution(6630288811907503637)
XLA Ops:
  0.0 1.6 %collective-permute-start.1 = (bf16[512,512]{1,0:T(8,128)(2,1)}, bf16[512,512]{1,0:T(8,128)(2,1)S(1)}, u32[]{:S(2)}, u32[]{:S(2)}) collective-permute-start(bf16[512,512]{1,0:T(8,128)(2,1)} %refs_10_), channel_id=1, source_target_pairs={{0,1},{1,2},{2,3},{3,0},{4,5},{5,6},{6,7},{7,4},{8,9},{9,10},{10,1... | collective-permute-start | bytes 1572872 | tf_op jit(solution)/shard_map/ppermute | solution.py:304
  1.6 1.9 %collective-permute-start = (bf16[512,512]{1,0:T(8,128)(2,1)}, bf16[512,512]{1,0:T(8,128)(2,1)}, u32[]{:S(2)}, u32[]{:S(2)}) collective-permute-start(bf16[512,512]{1,0:T(8,128)(2,1)} %refs_10_), channel_id=1, source_target_pairs={{0,4},{1,5},{2,6},{3,7},{4,8},{5,9},{6,10},{7,11},{8,12},{9,13},{1... | collective-permute-start | bytes 1572872 | tf_op jit(solution)/shard_map/ppermute | solution.py:308
  3.5 1.7 %collective-permute-start.2 = (bf16[512,512]{1,0:T(8,128)(2,1)}, bf16[512,512]{1,0:T(8,128)(2,1)}, u32[]{:S(2)}, u32[]{:S(2)}) collective-permute-start(bf16[512,512]{1,0:T(8,128)(2,1)} %refs_10_), channel_id=1, source_target_pairs={{0,3},{1,0},{2,1},{3,2},{4,7},{5,4},{6,5},{7,6},{8,11},{9,8},{10,9... | collective-permute-start | bytes 1572872 | tf_op jit(solution)/shard_map/ppermute | solution.py:304
  5.2 2.1 %collective-permute-start.3 = (bf16[512,512]{1,0:T(8,128)(2,1)}, bf16[512,512]{1,0:T(8,128)(2,1)}, u32[]{:S(2)}, u32[]{:S(2)}) collective-permute-start(bf16[512,512]{1,0:T(8,128)(2,1)} %refs_10_), channel_id=1, source_target_pairs={{0,12},{1,13},{2,14},{3,15},{4,0},{5,1},{6,2},{7,3},{8,4},{9,5},{1... | collective-permute-start | bytes 1572872 | tf_op jit(solution)/shard_map/ppermute | solution.py:308
  10.8 1.2 %shard_map.82 = bf16[128,40,128]{2,1,0:T(8,128)(2,1)} custom-call(bf16[128,16,128]{2,1,0:T(8,128)(2,1)S(1)} %bitcast.59, s32[16,128]{1,0:T(8,128)S(1)} %bitcast.60, s32[16,128]{1,0:T(8,128)S(1)} %bitcast.61, bf16[128,8,128]{2,1,0:T(8,128)(2,1)S(1)} %pad.4.corner), custom_call_target="tpu_custom_call" | custom-call | tf_op jit(solution)/shard_map/pallas_call | solution.py:359
  12.0 2.9 %collective-permute-done.1.refs_11_ = bf16[512,512]{1,0:T(8,128)(2,1)S(1)} collective-permute-done((bf16[512,512]{1,0:T(8,128)(2,1)}, bf16[512,512]{1,0:T(8,128)(2,1)S(1)}, u32[]{:S(2)}, u32[]{:S(2)}) %collective-permute-start.1) | collective-permute-done | bytes 524320 | tf_op jit(solution)/shard_map/ppermute | solution.py:304
  15.0 2.6 %collective-permute-done.refs_13_ = bf16[512,512]{1,0:T(8,128)(2,1)} collective-permute-done((bf16[512,512]{1,0:T(8,128)(2,1)}, bf16[512,512]{1,0:T(8,128)(2,1)}, u32[]{:S(2)}, u32[]{:S(2)}) %collective-permute-start) | collective-permute-done | bytes 524320 | tf_op jit(solution)/shard_map/ppermute | solution.py:308
  18.6 9.2 %all-to-all-start = ((bf16[128,40,128]{2,1,0:T(8,128)(2,1)}), bf16[128,40,128]{2,1,0:T(8,128)(2,1)S(1)}, u32[]{:S(2)}, u32[]{:S(2)}) async-start(bf16[128,40,128]{2,1,0:T(8,128)(2,1)} %shard_map.82), calls=%async_computation | async-start | bytes 2621440 | tf_op jit(solution)/shard_map/all_to_all | solution.py:367
  28.7 2.1 %fusion.w_tile.refs_6_ = bf16[512,2048]{1,0:T(8,128)(2,1)} fusion(bf16[512,256]{1,0:T(8,128)(2,1)S(1)} %copy-done, s32[2048]{0:T(1024)S(1)} %get-tuple-element.79, s32[2048]{0:T(1024)S(1)} %get-tuple-element.81, s32[2048]{0:T(1024)S(1)} %get-tuple-element.80, s32[2048]{0:T(1024)S(1)} %get-tuple-element.82, pred[2048]{0:T(1024)(128)(4,1)S(1)} %get-tuple-element.84, ...), kind=kOutput, calls=%fused_computation.1 | convolution fusion | flops 540540928 | bytes 2396160 | tf_op jit(solution)/shard_map/dot_general | solution.py:26
  30.9 2.8 %collective-permute-start.6 = (bf16[512,512]{1,0:T(8,128)(2,1)S(1)}, bf16[512,512]{1,0:T(8,128)(2,1)}, u32[]{:S(2)}, u32[]{:S(2)}) collective-permute-start(bf16[512,512]{1,0:T(8,128)(2,1)S(1)} %collective-permute-done.1.refs_11_), channel_id=1, source_target_pairs={{0,12},{1,13},{2,14},{3,15},{4,0},{5,1},{6,2},{7,3},{8,4},{9,5},{1... | collective-permute-start | bytes 1572872 | tf_op jit(solution)/shard_map/ppermute | solution.py:308
  33.7 1.5 %collective-permute-start.7 = (bf16[512,512]{1,0:T(8,128)(2,1)}, bf16[512,512]{1,0:T(8,128)(2,1)}, u32[]{:S(2)}, u32[]{:S(2)}) collective-permute-start(bf16[512,512]{1,0:T(8,128)(2,1)} %collective-permute-done.refs_13_), channel_id=1, source_target_pairs={{0,1},{1,2},{2,3},{3,0},{4,5},{5,6},{6,7},{7,4},{8,9},{9,10},{10,1... | collective-permute-start | bytes 1572872 | tf_op jit(solution)/shard_map/ppermute | solution.py:304
  35.2 1.8 %collective-permute-start.4 = (bf16[512,512]{1,0:T(8,128)(2,1)}, bf16[512,512]{1,0:T(8,128)(2,1)}, u32[]{:S(2)}, u32[]{:S(2)}) collective-permute-start(bf16[512,512]{1,0:T(8,128)(2,1)} %collective-permute-done.3.refs_14_), channel_id=1, source_target_pairs={{0,3},{1,0},{2,1},{3,2},{4,7},{5,4},{6,5},{7,6},{8,11},{9,8},{10,9... | collective-permute-start | bytes 1572872 | tf_op jit(solution)/shard_map/ppermute | solution.py:304
  36.9 12.7 %all-to-all-done.recv = bf16[128,40,128]{2,1,0:T(8,128)(2,1)S(1)} async-done(((bf16[128,40,128]{2,1,0:T(8,128)(2,1)}), bf16[128,40,128]{2,1,0:T(8,128)(2,1)S(1)}, u32[]{:S(2)}, u32[]{:S(2)}) %all-to-all-start) | async-done | bytes 1310752 | tf_op jit(solution)/shard_map/all_to_all | solution.py:367
  51.2 4.6 %all-to-all-start.1 = ((bf16[128,4,128]{2,1,0:T(4,128)(2,1)}), bf16[128,4,128]{2,1,0:T(4,128)(2,1)S(1)}, u32[]{:S(2)}, u32[]{:S(2)}) async-start(bf16[128,4,128]{2,1,0:T(4,128)(2,1)} %broadcast_in_dim.25), calls=%async_computation.1 | async-start | bytes 262144 | tf_op jit(solution)/shard_map/all_to_all | solution.py:369
  56.3 1.5 %collective-permute-done.5.refs_16_ = bf16[512,512]{1,0:T(8,128)(2,1)} collective-permute-done((bf16[512,512]{1,0:T(8,128)(2,1)}, bf16[512,512]{1,0:T(8,128)(2,1)}, u32[]{:S(2)}, u32[]{:S(2)}) %collective-permute-start.5) | collective-permute-done | bytes 524320 | tf_op jit(solution)/shard_map/ppermute | solution.py:308
  57.8 1.5 %collective-permute-start.10 = (bf16[512,512]{1,0:T(8,128)(2,1)S(1)}, bf16[512,512]{1,0:T(8,128)(2,1)}, u32[]{:S(2)}, u32[]{:S(2)}) collective-permute-start(bf16[512,512]{1,0:T(8,128)(2,1)S(1)} %collective-permute-done.1.refs_11_), channel_id=1, source_target_pairs={{0,1},{1,2},{2,3},{3,0},{4,5},{5,6},{6,7},{7,4},{8,9},{9,10},{10,1... | collective-permute-start | bytes 1572872 | tf_op jit(solution)/shard_map/ppermute | solution.py:304
  59.3 1.9 %collective-permute-start.8 = (bf16[512,512]{1,0:T(8,128)(2,1)}, bf16[512,512]{1,0:T(8,128)(2,1)}, u32[]{:S(2)}, u32[]{:S(2)}) collective-permute-start(bf16[512,512]{1,0:T(8,128)(2,1)} %collective-permute-done.4.refs_15_), channel_id=1, source_target_pairs={{0,3},{1,0},{2,1},{3,2},{4,7},{5,4},{6,5},{7,6},{8,11},{9,8},{10,9... | collective-permute-start | bytes 1572872 | tf_op jit(solution)/shard_map/ppermute | solution.py:304
  61.2 3.1 %collective-permute-start.9 = (bf16[512,512]{1,0:T(8,128)(2,1)}, bf16[512,512]{1,0:T(8,128)(2,1)}, u32[]{:S(2)}, u32[]{:S(2)}) collective-permute-start(bf16[512,512]{1,0:T(8,128)(2,1)} %collective-permute-done.6.refs_17_), channel_id=1, source_target_pairs={{0,12},{1,13},{2,14},{3,15},{4,0},{5,1},{6,2},{7,3},{8,4},{9,5},{1... | collective-permute-start | bytes 1572872 | tf_op jit(solution)/shard_map/ppermute | solution.py:308
  64.6 1.6 %copy-done.8 = bf16[512,2048]{1,0:T(8,128)(2,1)S(1)} copy-done((bf16[512,2048]{1,0:T(8,128)(2,1)S(1)}, bf16[512,2048]{1,0:T(8,128)(2,1)}, u32[]{:S(2)}) %copy-start.8) | copy-done | bytes 2097176
  66.2 7.0 %shard_map.83 = (bf16[2048,512]{1,0:T(8,128)(2,1)S(1)}, f32[2048,128]{1,0:T(8,128)S(1)}) custom-call(s32[16,128]{1,0:T(8,128)S(1)} %add.269.code, bf16[128,40,128]{2,1,0:T(8,128)(2,1)S(1)} %all-to-all-done.recv, bf16[128,512]{1,0:T(8,128)(2,1)S(1)} %copy-done.7, bf16[512,512]{1,0:T(8,128)(2,1)S(1)} %copy-done.6, bf16[512,2048]{1,0:T(8,128)(2,1)S(1)} %copy-done.8), custom_call_target="tpu_custom_call" | custom-call | flops 10000000000 | bytes 8000000 | tf_op jit(solution)/shard_map/pallas_call | solution.py:393
  73.1 1.3 %copy-done.9 = bf16[2048,512]{1,0:T(8,128)(2,1)} copy-done((bf16[2048,512]{1,0:T(8,128)(2,1)}, bf16[2048,512]{1,0:T(8,128)(2,1)S(1)}, u32[]{:S(2)}) %copy-start.9) | copy-done | bytes 2097176
  76.9 2.1 %collective-permute-start.13 = (bf16[512,512]{1,0:T(8,128)(2,1)}, bf16[512,512]{1,0:T(8,128)(2,1)S(1)}, u32[]{:S(2)}, u32[]{:S(2)}) collective-permute-start(bf16[512,512]{1,0:T(8,128)(2,1)} %collective-permute-done.4.refs_15_), channel_id=1, source_target_pairs={{0,12},{1,13},{2,14},{3,15},{4,0},{5,1},{6,2},{7,3},{8,4},{9,5},{1... | collective-permute-start | bytes 1572872 | tf_op jit(solution)/shard_map/ppermute | solution.py:308
  81.7 26.2 %shard_map.84 = (f32[8192,512]{1,0:T(8,128)}, bf16[512,512]{1,0:T(8,128)(2,1)}) custom-call(s32[17]{0:T(128)} %stack.75.refs_0_, s32[2048]{0:T(1024)} %fusion.28.refs_1_, s32[128]{0:T(128)} %copy-done.12, s32[8]{0:T(128)} %select_reduce_fusion.1.refs_3_, bf16[2048,512]{1,0:T(8,128)(2,1)} %copy-done.9, f32[128,16]{1,0:T(8,128)} %get-tuple-element.75.refs_5_, ...), custom_call_target="tpu_custom_call" | custom-call | flops 15000000512 | bytes 30000000 | tf_op jit(solution)/shard_map/pallas_call | solution.py:415
  109.0 4.3 %shard_map.85 = f32[8192,512]{1,0:T(8,128)} custom-call(s32[17]{0:T(128)S(1)} %copy-done.5, bf16[512,512]{1,0:T(8,128)(2,1)S(1)} %copy-done.1, f32[8192,512]{1,0:T(8,128)} %get-tuple-element.74.refs_2_, bf16[512,512]{1,0:T(8,128)(2,1)S(1)} %collective-permute-done.12.refs_3_, ...), custom_call_target="tpu_custom_call", output_to_operand_aliasing={{}: (2, {})} | custom-call | flops 800000000 | bytes 8000000 | tf_op jit(solution)/shard_map/pallas_call | solution.py:439
  (70 shorter events, 13.5 us)
Async XLA Ops:
  0.0 28.7 %copy-start = (bf16[512,256]{1,0:T(8,128)(2,1)S(1)}, bf16[512,256]{1,0:T(8,128)(2,1)}, u32[]{:S(2)}) copy-start(bf16[512,256]{1,0:T(8,128)(2,1)} %param.13) | copy-start | bytes 786436
  0.0 15.0 %collective-permute-start.1 = (bf16[512,512]{1,0:T(8,128)(2,1)}, bf16[512,512]{1,0:T(8,128)(2,1)S(1)}, u32[]{:S(2)}, u32[]{:S(2)}) collective-permute-start(bf16[512,512]{1,0:T(8,128)(2,1)} %refs_10_), channel_id=1, source_target_pairs={{0,1},{1,2},{2,3},{3,0},{4,5},{5,6},{6,7},{7,4},{8,9},{9,10},{10,1... | collective-permute-start | bytes 1572872 | tf_op jit(solution)/shard_map/ppermute | solution.py:304
  1.6 16.0 %collective-permute-start = (bf16[512,512]{1,0:T(8,128)(2,1)}, bf16[512,512]{1,0:T(8,128)(2,1)}, u32[]{:S(2)}, u32[]{:S(2)}) collective-permute-start(bf16[512,512]{1,0:T(8,128)(2,1)} %refs_10_), channel_id=1, source_target_pairs={{0,4},{1,5},{2,6},{3,7},{4,8},{5,9},{6,10},{7,11},{8,12},{9,13},{1... | collective-permute-start | bytes 1572872 | tf_op jit(solution)/shard_map/ppermute | solution.py:308
  3.5 14.1 %collective-permute-start.2 = (bf16[512,512]{1,0:T(8,128)(2,1)}, bf16[512,512]{1,0:T(8,128)(2,1)}, u32[]{:S(2)}, u32[]{:S(2)}) collective-permute-start(bf16[512,512]{1,0:T(8,128)(2,1)} %refs_10_), channel_id=1, source_target_pairs={{0,3},{1,0},{2,1},{3,2},{4,7},{5,4},{6,5},{7,6},{8,11},{9,8},{10,9... | collective-permute-start | bytes 1572872 | tf_op jit(solution)/shard_map/ppermute | solution.py:304
  5.2 13.3 %collective-permute-start.3 = (bf16[512,512]{1,0:T(8,128)(2,1)}, bf16[512,512]{1,0:T(8,128)(2,1)}, u32[]{:S(2)}, u32[]{:S(2)}) collective-permute-start(bf16[512,512]{1,0:T(8,128)(2,1)} %refs_10_), channel_id=1, source_target_pairs={{0,12},{1,13},{2,14},{3,15},{4,0},{5,1},{6,2},{7,3},{8,4},{9,5},{1... | collective-permute-start | bytes 1572872 | tf_op jit(solution)/shard_map/ppermute | solution.py:308
  15.0 42.8 %copy-start.13 = (bf16[512,512]{1,0:T(8,128)(2,1)}, bf16[512,512]{1,0:T(8,128)(2,1)S(1)}, u32[]{:S(2)}) copy-start(bf16[512,512]{1,0:T(8,128)(2,1)S(1)} %collective-permute-done.1.refs_11_) | copy-start | bytes 1572868
  18.6 31.0 %all-to-all-start = ((bf16[128,40,128]{2,1,0:T(8,128)(2,1)}), bf16[128,40,128]{2,1,0:T(8,128)(2,1)S(1)}, u32[]{:S(2)}, u32[]{:S(2)}) async-start(bf16[128,40,128]{2,1,0:T(8,128)(2,1)} %shard_map.82), calls=%async_computation | async-start | bytes 2621440 | tf_op jit(solution)/shard_map/all_to_all | solution.py:367
  28.7 35.9 %copy-start.6 = (bf16[512,512]{1,0:T(8,128)(2,1)S(1)}, bf16[512,512]{1,0:T(8,128)(2,1)}, u32[]{:S(2)}) copy-start(bf16[512,512]{1,0:T(8,128)(2,1)} %w_mid.1) | copy-start | bytes 1572868
  28.7 35.9 %copy-start.7 = (bf16[128,512]{1,0:T(8,128)(2,1)S(1)}, bf16[128,512]{1,0:T(8,128)(2,1)}, u32[]{:S(2)}) copy-start(bf16[128,512]{1,0:T(8,128)(2,1)} %w_in.1) | copy-start | bytes 393220
  30.9 25.5 %collective-permute-start.6 = (bf16[512,512]{1,0:T(8,128)(2,1)S(1)}, bf16[512,512]{1,0:T(8,128)(2,1)}, u32[]{:S(2)}, u32[]{:S(2)}) collective-permute-start(bf16[512,512]{1,0:T(8,128)(2,1)S(1)} %collective-permute-done.1.refs_11_), channel_id=1, source_target_pairs={{0,12},{1,13},{2,14},{3,15},{4,0},{5,1},{6,2},{7,3},{8,4},{9,5},{1... | collective-permute-start | bytes 1572872 | tf_op jit(solution)/shard_map/ppermute | solution.py:308
  33.7 24.1 %collective-permute-start.5 = (bf16[512,512]{1,0:T(8,128)(2,1)}, bf16[512,512]{1,0:T(8,128)(2,1)}, u32[]{:S(2)}, u32[]{:S(2)}) collective-permute-start(bf16[512,512]{1,0:T(8,128)(2,1)} %collective-permute-done.2.refs_12_), channel_id=1, source_target_pairs={{0,4},{1,5},{2,6},{3,7},{4,8},{5,9},{6,10},{7,11},{8,12},{9,13},{1... | collective-permute-start | bytes 1572872 | tf_op jit(solution)/shard_map/ppermute | solution.py:308
  33.7 24.1 %collective-permute-start.7 = (bf16[512,512]{1,0:T(8,128)(2,1)}, bf16[512,512]{1,0:T(8,128)(2,1)}, u32[]{:S(2)}, u32[]{:S(2)}) collective-permute-start(bf16[512,512]{1,0:T(8,128)(2,1)} %collective-permute-done.refs_13_), channel_id=1, source_target_pairs={{0,1},{1,2},{2,3},{3,0},{4,5},{5,6},{6,7},{7,4},{8,9},{9,10},{10,1... | collective-permute-start | bytes 1572872 | tf_op jit(solution)/shard_map/ppermute | solution.py:304
  35.2 22.6 %collective-permute-start.4 = (bf16[512,512]{1,0:T(8,128)(2,1)}, bf16[512,512]{1,0:T(8,128)(2,1)}, u32[]{:S(2)}, u32[]{:S(2)}) collective-permute-start(bf16[512,512]{1,0:T(8,128)(2,1)} %collective-permute-done.3.refs_14_), channel_id=1, source_target_pairs={{0,3},{1,0},{2,1},{3,2},{4,7},{5,4},{6,5},{7,6},{8,11},{9,8},{10,9... | collective-permute-start | bytes 1572872 | tf_op jit(solution)/shard_map/ppermute | solution.py:304
  51.2 29.8 %all-to-all-start.1 = ((bf16[128,4,128]{2,1,0:T(4,128)(2,1)}), bf16[128,4,128]{2,1,0:T(4,128)(2,1)S(1)}, u32[]{:S(2)}, u32[]{:S(2)}) async-start(bf16[128,4,128]{2,1,0:T(4,128)(2,1)} %broadcast_in_dim.25), calls=%async_computation.1 | async-start | bytes 262144 | tf_op jit(solution)/shard_map/all_to_all | solution.py:369
  57.8 19.0 %collective-permute-start.10 = (bf16[512,512]{1,0:T(8,128)(2,1)S(1)}, bf16[512,512]{1,0:T(8,128)(2,1)}, u32[]{:S(2)}, u32[]{:S(2)}) collective-permute-start(bf16[512,512]{1,0:T(8,128)(2,1)S(1)} %collective-permute-done.1.refs_11_), channel_id=1, source_target_pairs={{0,1},{1,2},{2,3},{3,0},{4,5},{5,6},{6,7},{7,4},{8,9},{9,10},{10,1... | collective-permute-start | bytes 1572872 | tf_op jit(solution)/shard_map/ppermute | solution.py:304
  59.3 17.6 %collective-permute-start.11 = (bf16[512,512]{1,0:T(8,128)(2,1)}, bf16[512,512]{1,0:T(8,128)(2,1)}, u32[]{:S(2)}, u32[]{:S(2)}) collective-permute-start(bf16[512,512]{1,0:T(8,128)(2,1)} %collective-permute-done.refs_13_), channel_id=1, source_target_pairs={{0,4},{1,5},{2,6},{3,7},{4,8},{5,9},{6,10},{7,11},{8,12},{9,13},{1... | collective-permute-start | bytes 1572872 | tf_op jit(solution)/shard_map/ppermute | solution.py:308
  59.3 17.6 %collective-permute-start.8 = (bf16[512,512]{1,0:T(8,128)(2,1)}, bf16[512,512]{1,0:T(8,128)(2,1)}, u32[]{:S(2)}, u32[]{:S(2)}) collective-permute-start(bf16[512,512]{1,0:T(8,128)(2,1)} %collective-permute-done.4.refs_15_), channel_id=1, source_target_pairs={{0,3},{1,0},{2,1},{3,2},{4,7},{5,4},{6,5},{7,6},{8,11},{9,8},{10,9... | collective-permute-start | bytes 1572872 | tf_op jit(solution)/shard_map/ppermute | solution.py:304
  61.2 15.6 %collective-permute-start.9 = (bf16[512,512]{1,0:T(8,128)(2,1)}, bf16[512,512]{1,0:T(8,128)(2,1)}, u32[]{:S(2)}, u32[]{:S(2)}) collective-permute-start(bf16[512,512]{1,0:T(8,128)(2,1)} %collective-permute-done.6.refs_17_), channel_id=1, source_target_pairs={{0,12},{1,13},{2,14},{3,15},{4,0},{5,1},{6,2},{7,3},{8,4},{9,5},{1... | collective-permute-start | bytes 1572872 | tf_op jit(solution)/shard_map/ppermute | solution.py:308
  64.6 1.6 %copy-start.8 = (bf16[512,2048]{1,0:T(8,128)(2,1)S(1)}, bf16[512,2048]{1,0:T(8,128)(2,1)}, u32[]{:S(2)}) copy-start(bf16[512,2048]{1,0:T(8,128)(2,1)} %fusion.w_tile.refs_6_) | copy-start | bytes 6291460
  66.2 9.9 %copy-start.12 = (s32[128]{0:T(128)}, s32[128]{0:T(128)S(1)}, u32[]{:S(2)}) copy-start(s32[128]{0:T(128)S(1)} %select_reduce_fusion.refs_2_) | copy-start | bytes 1540
  76.9 31.0 %collective-permute-start.13 = (bf16[512,512]{1,0:T(8,128)(2,1)}, bf16[512,512]{1,0:T(8,128)(2,1)S(1)}, u32[]{:S(2)}, u32[]{:S(2)}) collective-permute-start(bf16[512,512]{1,0:T(8,128)(2,1)} %collective-permute-done.4.refs_15_), channel_id=1, source_target_pairs={{0,12},{1,13},{2,14},{3,15},{4,0},{5,1},{6,2},{7,3},{8,4},{9,5},{1... | collective-permute-start | bytes 1572872 | tf_op jit(solution)/shard_map/ppermute | solution.py:308
  79.0 28.9 %collective-permute-start.12 = (bf16[512,512]{1,0:T(8,128)(2,1)}, bf16[512,512]{1,0:T(8,128)(2,1)S(1)}, u32[]{:S(2)}, u32[]{:S(2)}) collective-permute-start(bf16[512,512]{1,0:T(8,128)(2,1)} %collective-permute-done.5.refs_16_), channel_id=1, source_target_pairs={{0,3},{1,0},{2,1},{3,2},{4,7},{5,4},{6,5},{7,6},{8,11},{9,8},{10,9... | collective-permute-start | bytes 1572872 | tf_op jit(solution)/shard_map/ppermute | solution.py:304
  80.1 27.8 %collective-permute-start.14 = (bf16[512,512]{1,0:T(8,128)(2,1)}, bf16[512,512]{1,0:T(8,128)(2,1)S(1)}, u32[]{:S(2)}, u32[]{:S(2)}) collective-permute-start(bf16[512,512]{1,0:T(8,128)(2,1)} %collective-permute-done.9.refs_20_), channel_id=1, source_target_pairs={{0,1},{1,2},{2,3},{3,0},{4,5},{5,6},{6,7},{7,4},{8,9},{9,10},{10,1... | collective-permute-start | bytes 1572872 | tf_op jit(solution)/shard_map/ppermute | solution.py:304
  81.7 26.3 %copy-start.5 = (s32[17]{0:T(128)S(1)}, s32[17]{0:T(128)}, u32[]{:S(2)}) copy-start(s32[17]{0:T(128)} %stack.75.refs_0_) | copy-start | bytes 208
  (7 other events, 6.5 us)

commit v3 on v2

--- a/solution.py
+++ b/solution.py
@@ -141,7 +141,7 @@
         slab[pl.ds(pl.multiple_of(i * 512, 512), 512), :] = jnp.zeros((512, LANES), F32)
         return carry
 
-    lax.fori_loop(0, slab.shape[0] // 512, clear, 0)
+    lax.fori_loop(0, slab.shape[0] // 512, clear, 0, unroll=2)
     for copy in early:
         copy.wait()
 
@@ -182,7 +182,7 @@
             lax.while_loop(some, one, lost[k * peers + peer])
             return bits & (bits - 1)
 
-        lax.fori_loop(0, CHUNK // SET, place, 0)
+        lax.fori_loop(0, CHUNK // SET, place, 0, unroll=4)
         lax.while_loop(some, repair, clashes[k])
         return carry
 
@@ -411,7 +411,6 @@
     place = jnp.stack(place + [(lax.axis_index("row") == 0).astype(jnp.int32)]).astype(jnp.int32)
     count = len(got)
     pieces = list(got.values())
-    held = [pltpu.with_memory_space_constraint(value, pltpu.HBM) for value in pieces[:ready]]
     part, solved_b = pl.pallas_call(
         functools.partial(final_kernel, ready),
         out_shape=(
@@ -434,7 +433,7 @@
         ],
         compiler_params=pltpu.CompilerParams(vmem_limit_bytes=56 * MIB),
         cost_estimate=pl.CostEstimate(flops=15_000_000_000, bytes_accessed=30_000_000, transcendentals=0),
-    )(place, dest, lost, clashes, two, lane, w_tile, head, diag_inverse, corner, *held)
+    )(place, dest, lost, clashes, two, lane, w_tile, head, diag_inverse, corner, *pieces[:ready])
     left = count - ready
     return pl.pallas_call(
         functools.partial(last_kernel, ready),

time: 114 us -> 113 us (level)
    pallas_call x1, Pallas kernels: 26.2 us -> 25.1 us  [body(): pl.pallas_call(functools.partial(final_kernel, ready), out_shape=(jax.Sha...]
where the time goes in v3:
time: 113 us; the launch traced here: 112 us
  starting transfers between devices  38 us (34%)
  Pallas kernels  37.5 us (33%)
  waiting for transfers between devices  20.7 us (18%)
  local copies, waits for them, and re-layouts  10.8 us (10%)
  other arithmetic  2.48 us (2%)
  matrix products  2.14 us (2%)
    pallas_call x1, Pallas kernels, body(): pl.pallas_call(functools.partial(final_kernel, ready), out_shape=(jax.Sha...  25.1 us
    all_to_all x1, waiting for transfers between devices, body(): recv = lax.all_to_all(payload, ('row', 'col'), 0, 0, tiled=True)  12.7 us
    ppermute x7, starting transfers between devices, along_z(): lax.ppermute(value, 'col', [(z * 4 + x, (z + by) % 4 * 4 + x) for z in ra...  12.1 us
    ppermute x8, starting transfers between devices, along_x(): lax.ppermute(value, 'col', [(z * 4 + x, z * 4 + (x + by) % 4) for z in ra...  12 us
    all_to_all x1, starting transfers between devices, body(): recv = lax.all_to_all(payload, ('row', 'col'), 0, 0, tiled=True)  9.22 us
    unnamed x28, local copies, waits for them, and re-layouts  8.05 us
    pallas_call x1, Pallas kernels, body(): pl.pallas_call(hidden_kernel, out_shape=(jax.ShapeDtypeStruct((16 * peers...  6.95 us
    ppermute x7, waiting for transfers between devices, along_z(): lax.ppermute(value, 'col', [(z * 4 + x, (z + by) % 4 * 4 + x) for z in ra...  5.08 us
  transfers between devices with their start and end apart: 17, of which 5 were waited for; matrix products, arithmetic and copies ran while one was open for 7% of the time, Pallas kernels for 30%

profile of v3, /device:TPU:0, one launch (start us, length us, event | category | flops | bytes accessed | tf_op | source)
XLA Modules:
  0.0 112.2 jit_solution(10575804569463541010)
XLA Ops:
  0.0 1.6 %collective-permute-start.1 = (bf16[512,512]{1,0:T(8,128)(2,1)}, bf16[512,512]{1,0:T(8,128)(2,1)S(1)}, u32[]{:S(2)}, u32[]{:S(2)}) collective-permute-start(bf16[512,512]{1,0:T(8,128)(2,1)} %refs_10_), channel_id=1, source_target_pairs={{0,1},{1,2},{2,3},{3,0},{4,5},{5,6},{6,7},{7,4},{8,9},{9,10},{10,1... | collective-permute-start | bytes 1572872 | tf_op jit(solution)/shard_map/ppermute | solution.py:304
  1.6 1.9 %collective-permute-start = (bf16[512,512]{1,0:T(8,128)(2,1)}, bf16[512,512]{1,0:T(8,128)(2,1)}, u32[]{:S(2)}, u32[]{:S(2)}) collective-permute-start(bf16[512,512]{1,0:T(8,128)(2,1)} %refs_10_), channel_id=1, source_target_pairs={{0,4},{1,5},{2,6},{3,7},{4,8},{5,9},{6,10},{7,11},{8,12},{9,13},{1... | collective-permute-start | bytes 1572872 | tf_op jit(solution)/shard_map/ppermute | solution.py:308
  3.5 1.7 %collective-permute-start.2 = (bf16[512,512]{1,0:T(8,128)(2,1)}, bf16[512,512]{1,0:T(8,128)(2,1)}, u32[]{:S(2)}, u32[]{:S(2)}) collective-permute-start(bf16[512,512]{1,0:T(8,128)(2,1)} %refs_10_), channel_id=1, source_target_pairs={{0,3},{1,0},{2,1},{3,2},{4,7},{5,4},{6,5},{7,6},{8,11},{9,8},{10,9... | collective-permute-start | bytes 1572872 | tf_op jit(solution)/shard_map/ppermute | solution.py:304
  5.2 2.1 %collective-permute-start.3 = (bf16[512,512]{1,0:T(8,128)(2,1)}, bf16[512,512]{1,0:T(8,128)(2,1)}, u32[]{:S(2)}, u32[]{:S(2)}) collective-permute-start(bf16[512,512]{1,0:T(8,128)(2,1)} %refs_10_), channel_id=1, source_target_pairs={{0,12},{1,13},{2,14},{3,15},{4,0},{5,1},{6,2},{7,3},{8,4},{9,5},{1... | collective-permute-start | bytes 1572872 | tf_op jit(solution)/shard_map/ppermute | solution.py:308
  10.8 1.2 %shard_map.82 = bf16[128,40,128]{2,1,0:T(8,128)(2,1)} custom-call(bf16[128,16,128]{2,1,0:T(8,128)(2,1)S(1)} %bitcast.59, s32[16,128]{1,0:T(8,128)S(1)} %bitcast.60, s32[16,128]{1,0:T(8,128)S(1)} %bitcast.61, bf16[128,8,128]{2,1,0:T(8,128)(2,1)S(1)} %pad.4.corner), custom_call_target="tpu_custom_call" | custom-call | tf_op jit(solution)/shard_map/pallas_call | solution.py:359
  12.0 2.9 %collective-permute-done.1.refs_11_ = bf16[512,512]{1,0:T(8,128)(2,1)S(1)} collective-permute-done((bf16[512,512]{1,0:T(8,128)(2,1)}, bf16[512,512]{1,0:T(8,128)(2,1)S(1)}, u32[]{:S(2)}, u32[]{:S(2)}) %collective-permute-start.1) | collective-permute-done | bytes 524320 | tf_op jit(solution)/shard_map/ppermute | solution.py:304
  15.0 2.6 %collective-permute-done.refs_13_ = bf16[512,512]{1,0:T(8,128)(2,1)} collective-permute-done((bf16[512,512]{1,0:T(8,128)(2,1)}, bf16[512,512]{1,0:T(8,128)(2,1)}, u32[]{:S(2)}, u32[]{:S(2)}) %collective-permute-start) | collective-permute-done | bytes 524320 | tf_op jit(solution)/shard_map/ppermute | solution.py:308
  18.6 9.2 %all-to-all-start = ((bf16[128,40,128]{2,1,0:T(8,128)(2,1)}), bf16[128,40,128]{2,1,0:T(8,128)(2,1)S(1)}, u32[]{:S(2)}, u32[]{:S(2)}) async-start(bf16[128,40,128]{2,1,0:T(8,128)(2,1)} %shard_map.82), calls=%async_computation | async-start | bytes 2621440 | tf_op jit(solution)/shard_map/all_to_all | solution.py:367
  28.7 2.1 %fusion.w_tile.refs_6_ = bf16[512,2048]{1,0:T(8,128)(2,1)} fusion(bf16[512,256]{1,0:T(8,128)(2,1)S(1)} %copy-done, s32[2048]{0:T(1024)S(1)} %get-tuple-element.79, s32[2048]{0:T(1024)S(1)} %get-tuple-element.81, s32[2048]{0:T(1024)S(1)} %get-tuple-element.80, s32[2048]{0:T(1024)S(1)} %get-tuple-element.82, pred[2048]{0:T(1024)(128)(4,1)S(1)} %get-tuple-element.84, ...), kind=kOutput, calls=%fused_computation.1 | convolution fusion | flops 540540928 | bytes 2396160 | tf_op jit(solution)/shard_map/dot_general | solution.py:26
  30.9 2.8 %collective-permute-start.6 = (bf16[512,512]{1,0:T(8,128)(2,1)S(1)}, bf16[512,512]{1,0:T(8,128)(2,1)}, u32[]{:S(2)}, u32[]{:S(2)}) collective-permute-start(bf16[512,512]{1,0:T(8,128)(2,1)S(1)} %collective-permute-done.1.refs_11_), channel_id=1, source_target_pairs={{0,12},{1,13},{2,14},{3,15},{4,0},{5,1},{6,2},{7,3},{8,4},{9,5},{1... | collective-permute-start | bytes 1572872 | tf_op jit(solution)/shard_map/ppermute | solution.py:308
  33.7 1.5 %collective-permute-start.7 = (bf16[512,512]{1,0:T(8,128)(2,1)}, bf16[512,512]{1,0:T(8,128)(2,1)}, u32[]{:S(2)}, u32[]{:S(2)}) collective-permute-start(bf16[512,512]{1,0:T(8,128)(2,1)} %collective-permute-done.refs_13_), channel_id=1, source_target_pairs={{0,1},{1,2},{2,3},{3,0},{4,5},{5,6},{6,7},{7,4},{8,9},{9,10},{10,1... | collective-permute-start | bytes 1572872 | tf_op jit(solution)/shard_map/ppermute | solution.py:304
  35.2 1.8 %collective-permute-start.4 = (bf16[512,512]{1,0:T(8,128)(2,1)}, bf16[512,512]{1,0:T(8,128)(2,1)}, u32[]{:S(2)}, u32[]{:S(2)}) collective-permute-start(bf16[512,512]{1,0:T(8,128)(2,1)} %collective-permute-done.3.refs_14_), channel_id=1, source_target_pairs={{0,3},{1,0},{2,1},{3,2},{4,7},{5,4},{6,5},{7,6},{8,11},{9,8},{10,9... | collective-permute-start | bytes 1572872 | tf_op jit(solution)/shard_map/ppermute | solution.py:304
  36.9 12.7 %all-to-all-done.recv = bf16[128,40,128]{2,1,0:T(8,128)(2,1)S(1)} async-done(((bf16[128,40,128]{2,1,0:T(8,128)(2,1)}), bf16[128,40,128]{2,1,0:T(8,128)(2,1)S(1)}, u32[]{:S(2)}, u32[]{:S(2)}) %all-to-all-start) | async-done | bytes 1310752 | tf_op jit(solution)/shard_map/all_to_all | solution.py:367
  51.2 4.6 %all-to-all-start.1 = ((bf16[128,4,128]{2,1,0:T(4,128)(2,1)}), bf16[128,4,128]{2,1,0:T(4,128)(2,1)S(1)}, u32[]{:S(2)}, u32[]{:S(2)}) async-start(bf16[128,4,128]{2,1,0:T(4,128)(2,1)} %broadcast_in_dim.25), calls=%async_computation.1 | async-start | bytes 262144 | tf_op jit(solution)/shard_map/all_to_all | solution.py:369
  56.3 1.5 %collective-permute-done.5.refs_16_ = bf16[512,512]{1,0:T(8,128)(2,1)} collective-permute-done((bf16[512,512]{1,0:T(8,128)(2,1)}, bf16[512,512]{1,0:T(8,128)(2,1)}, u32[]{:S(2)}, u32[]{:S(2)}) %collective-permute-start.5) | collective-permute-done | bytes 524320 | tf_op jit(solution)/shard_map/ppermute | solution.py:308
  57.8 1.5 %collective-permute-start.10 = (bf16[512,512]{1,0:T(8,128)(2,1)S(1)}, bf16[512,512]{1,0:T(8,128)(2,1)}, u32[]{:S(2)}, u32[]{:S(2)}) collective-permute-start(bf16[512,512]{1,0:T(8,128)(2,1)S(1)} %collective-permute-done.1.refs_11_), channel_id=1, source_target_pairs={{0,1},{1,2},{2,3},{3,0},{4,5},{5,6},{6,7},{7,4},{8,9},{9,10},{10,1... | collective-permute-start | bytes 1572872 | tf_op jit(solution)/shard_map/ppermute | solution.py:304
  59.3 1.9 %collective-permute-start.8 = (bf16[512,512]{1,0:T(8,128)(2,1)}, bf16[512,512]{1,0:T(8,128)(2,1)}, u32[]{:S(2)}, u32[]{:S(2)}) collective-permute-start(bf16[512,512]{1,0:T(8,128)(2,1)} %collective-permute-done.4.refs_15_), channel_id=1, source_target_pairs={{0,3},{1,0},{2,1},{3,2},{4,7},{5,4},{6,5},{7,6},{8,11},{9,8},{10,9... | collective-permute-start | bytes 1572872 | tf_op jit(solution)/shard_map/ppermute | solution.py:304
  61.2 3.1 %collective-permute-start.9 = (bf16[512,512]{1,0:T(8,128)(2,1)}, bf16[512,512]{1,0:T(8,128)(2,1)}, u32[]{:S(2)}, u32[]{:S(2)}) collective-permute-start(bf16[512,512]{1,0:T(8,128)(2,1)} %collective-permute-done.6.refs_17_), channel_id=1, source_target_pairs={{0,12},{1,13},{2,14},{3,15},{4,0},{5,1},{6,2},{7,3},{8,4},{9,5},{1... | collective-permute-start | bytes 1572872 | tf_op jit(solution)/shard_map/ppermute | solution.py:308
  64.6 1.6 %copy-done.8 = bf16[512,2048]{1,0:T(8,128)(2,1)S(1)} copy-done((bf16[512,2048]{1,0:T(8,128)(2,1)S(1)}, bf16[512,2048]{1,0:T(8,128)(2,1)}, u32[]{:S(2)}) %copy-start.8) | copy-done | bytes 2097176
  66.2 7.0 %shard_map.83 = (bf16[2048,512]{1,0:T(8,128)(2,1)S(1)}, f32[2048,128]{1,0:T(8,128)S(1)}) custom-call(s32[16,128]{1,0:T(8,128)S(1)} %add.269.code, bf16[128,40,128]{2,1,0:T(8,128)(2,1)S(1)} %all-to-all-done.recv, bf16[128,512]{1,0:T(8,128)(2,1)S(1)} %copy-done.7, bf16[512,512]{1,0:T(8,128)(2,1)S(1)} %copy-done.6, bf16[512,2048]{1,0:T(8,128)(2,1)S(1)} %copy-done.8), custom_call_target="tpu_custom_call" | custom-call | flops 10000000000 | bytes 8000000 | tf_op jit(solution)/shard_map/pallas_call | solution.py:393
  73.1 1.3 %copy-done.9 = bf16[2048,512]{1,0:T(8,128)(2,1)} copy-done((bf16[2048,512]{1,0:T(8,128)(2,1)}, bf16[2048,512]{1,0:T(8,128)(2,1)S(1)}, u32[]{:S(2)}) %copy-start.9) | copy-done | bytes 2097176
  76.9 2.1 %collective-permute-start.13 = (bf16[512,512]{1,0:T(8,128)(2,1)}, bf16[512,512]{1,0:T(8,128)(2,1)S(1)}, u32[]{:S(2)}, u32[]{:S(2)}) collective-permute-start(bf16[512,512]{1,0:T(8,128)(2,1)} %collective-permute-done.4.refs_15_), channel_id=1, source_target_pairs={{0,12},{1,13},{2,14},{3,15},{4,0},{5,1},{6,2},{7,3},{8,4},{9,5},{1... | collective-permute-start | bytes 1572872 | tf_op jit(solution)/shard_map/ppermute | solution.py:308
  81.7 25.1 %shard_map.84 = (f32[8192,512]{1,0:T(8,128)}, bf16[512,512]{1,0:T(8,128)(2,1)}) custom-call(s32[17]{0:T(128)} %stack.75.refs_0_, s32[2048]{0:T(1024)} %fusion.28.refs_1_, s32[128]{0:T(128)} %copy-done.12, s32[8]{0:T(128)} %select_reduce_fusion.1.refs_3_, bf16[2048,512]{1,0:T(8,128)(2,1)} %copy-done.9, f32[128,16]{1,0:T(8,128)} %get-tuple-element.75.refs_5_, ...), custom_call_target="tpu_custom_call" | custom-call | flops 15000000512 | bytes 30000000 | tf_op jit(solution)/shard_map/pallas_call | solution.py:414
  107.8 4.3 %shard_map.85 = f32[8192,512]{1,0:T(8,128)} custom-call(s32[17]{0:T(128)S(1)} %copy-done.5, bf16[512,512]{1,0:T(8,128)(2,1)S(1)} %copy-done.1, f32[8192,512]{1,0:T(8,128)} %get-tuple-element.74.refs_2_, bf16[512,512]{1,0:T(8,128)(2,1)S(1)} %collective-permute-done.12.refs_3_, ...), custom_call_target="tpu_custom_call", output_to_operand_aliasing={{}: (2, {})} | custom-call | flops 800000000 | bytes 8000000 | tf_op jit(solution)/shard_map/pallas_call | solution.py:438
  (70 shorter events, 13.5 us)
Async XLA Ops:
  0.0 28.7 %copy-start = (bf16[512,256]{1,0:T(8,128)(2,1)S(1)}, bf16[512,256]{1,0:T(8,128)(2,1)}, u32[]{:S(2)}) copy-start(bf16[512,256]{1,0:T(8,128)(2,1)} %param.13) | copy-start | bytes 786436
  0.0 15.0 %collective-permute-start.1 = (bf16[512,512]{1,0:T(8,128)(2,1)}, bf16[512,512]{1,0:T(8,128)(2,1)S(1)}, u32[]{:S(2)}, u32[]{:S(2)}) collective-permute-start(bf16[512,512]{1,0:T(8,128)(2,1)} %refs_10_), channel_id=1, source_target_pairs={{0,1},{1,2},{2,3},{3,0},{4,5},{5,6},{6,7},{7,4},{8,9},{9,10},{10,1... | collective-permute-start | bytes 1572872 | tf_op jit(solution)/shard_map/ppermute | solution.py:304
  1.6 16.0 %collective-permute-start = (bf16[512,512]{1,0:T(8,128)(2,1)}, bf16[512,512]{1,0:T(8,128)(2,1)}, u32[]{:S(2)}, u32[]{:S(2)}) collective-permute-start(bf16[512,512]{1,0:T(8,128)(2,1)} %refs_10_), channel_id=1, source_target_pairs={{0,4},{1,5},{2,6},{3,7},{4,8},{5,9},{6,10},{7,11},{8,12},{9,13},{1... | collective-permute-start | bytes 1572872 | tf_op jit(solution)/shard_map/ppermute | solution.py:308
  3.5 14.1 %collective-permute-start.2 = (bf16[512,512]{1,0:T(8,128)(2,1)}, bf16[512,512]{1,0:T(8,128)(2,1)}, u32[]{:S(2)}, u32[]{:S(2)}) collective-permute-start(bf16[512,512]{1,0:T(8,128)(2,1)} %refs_10_), channel_id=1, source_target_pairs={{0,3},{1,0},{2,1},{3,2},{4,7},{5,4},{6,5},{7,6},{8,11},{9,8},{10,9... | collective-permute-start | bytes 1572872 | tf_op jit(solution)/shard_map/ppermute | solution.py:304
  5.2 13.3 %collective-permute-start.3 = (bf16[512,512]{1,0:T(8,128)(2,1)}, bf16[512,512]{1,0:T(8,128)(2,1)}, u32[]{:S(2)}, u32[]{:S(2)}) collective-permute-start(bf16[512,512]{1,0:T(8,128)(2,1)} %refs_10_), channel_id=1, source_target_pairs={{0,12},{1,13},{2,14},{3,15},{4,0},{5,1},{6,2},{7,3},{8,4},{9,5},{1... | collective-permute-start | bytes 1572872 | tf_op jit(solution)/shard_map/ppermute | solution.py:308
  15.0 42.8 %copy-start.13 = (bf16[512,512]{1,0:T(8,128)(2,1)}, bf16[512,512]{1,0:T(8,128)(2,1)S(1)}, u32[]{:S(2)}) copy-start(bf16[512,512]{1,0:T(8,128)(2,1)S(1)} %collective-permute-done.1.refs_11_) | copy-start | bytes 1572868
  18.6 31.0 %all-to-all-start = ((bf16[128,40,128]{2,1,0:T(8,128)(2,1)}), bf16[128,40,128]{2,1,0:T(8,128)(2,1)S(1)}, u32[]{:S(2)}, u32[]{:S(2)}) async-start(bf16[128,40,128]{2,1,0:T(8,128)(2,1)} %shard_map.82), calls=%async_computation | async-start | bytes 2621440 | tf_op jit(solution)/shard_map/all_to_all | solution.py:367
  28.7 35.9 %copy-start.6 = (bf16[512,512]{1,0:T(8,128)(2,1)S(1)}, bf16[512,512]{1,0:T(8,128)(2,1)}, u32[]{:S(2)}) copy-start(bf16[512,512]{1,0:T(8,128)(2,1)} %w_mid.1) | copy-start | bytes 1572868
  28.7 35.9 %copy-start.7 = (bf16[128,512]{1,0:T(8,128)(2,1)S(1)}, bf16[128,512]{1,0:T(8,128)(2,1)}, u32[]{:S(2)}) copy-start(bf16[128,512]{1,0:T(8,128)(2,1)} %w_in.1) | copy-start | bytes 393220
  30.9 25.5 %collective-permute-start.6 = (bf16[512,512]{1,0:T(8,128)(2,1)S(1)}, bf16[512,512]{1,0:T(8,128)(2,1)}, u32[]{:S(2)}, u32[]{:S(2)}) collective-permute-start(bf16[512,512]{1,0:T(8,128)(2,1)S(1)} %collective-permute-done.1.refs_11_), channel_id=1, source_target_pairs={{0,12},{1,13},{2,14},{3,15},{4,0},{5,1},{6,2},{7,3},{8,4},{9,5},{1... | collective-permute-start | bytes 1572872 | tf_op jit(solution)/shard_map/ppermute | solution.py:308
  33.7 24.1 %collective-permute-start.5 = (bf16[512,512]{1,0:T(8,128)(2,1)}, bf16[512,512]{1,0:T(8,128)(2,1)}, u32[]{:S(2)}, u32[]{:S(2)}) collective-permute-start(bf16[512,512]{1,0:T(8,128)(2,1)} %collective-permute-done.2.refs_12_), channel_id=1, source_target_pairs={{0,4},{1,5},{2,6},{3,7},{4,8},{5,9},{6,10},{7,11},{8,12},{9,13},{1... | collective-permute-start | bytes 1572872 | tf_op jit(solution)/shard_map/ppermute | solution.py:308
  33.7 24.1 %collective-permute-start.7 = (bf16[512,512]{1,0:T(8,128)(2,1)}, bf16[512,512]{1,0:T(8,128)(2,1)}, u32[]{:S(2)}, u32[]{:S(2)}) collective-permute-start(bf16[512,512]{1,0:T(8,128)(2,1)} %collective-permute-done.refs_13_), channel_id=1, source_target_pairs={{0,1},{1,2},{2,3},{3,0},{4,5},{5,6},{6,7},{7,4},{8,9},{9,10},{10,1... | collective-permute-start | bytes 1572872 | tf_op jit(solution)/shard_map/ppermute | solution.py:304
  35.2 22.6 %collective-permute-start.4 = (bf16[512,512]{1,0:T(8,128)(2,1)}, bf16[512,512]{1,0:T(8,128)(2,1)}, u32[]{:S(2)}, u32[]{:S(2)}) collective-permute-start(bf16[512,512]{1,0:T(8,128)(2,1)} %collective-permute-done.3.refs_14_), channel_id=1, source_target_pairs={{0,3},{1,0},{2,1},{3,2},{4,7},{5,4},{6,5},{7,6},{8,11},{9,8},{10,9... | collective-permute-start | bytes 1572872 | tf_op jit(solution)/shard_map/ppermute | solution.py:304
  51.2 29.8 %all-to-all-start.1 = ((bf16[128,4,128]{2,1,0:T(4,128)(2,1)}), bf16[128,4,128]{2,1,0:T(4,128)(2,1)S(1)}, u32[]{:S(2)}, u32[]{:S(2)}) async-start(bf16[128,4,128]{2,1,0:T(4,128)(2,1)} %broadcast_in_dim.25), calls=%async_computation.1 | async-start | bytes 262144 | tf_op jit(solution)/shard_map/all_to_all | solution.py:369
  57.8 19.0 %collective-permute-start.10 = (bf16[512,512]{1,0:T(8,128)(2,1)S(1)}, bf16[512,512]{1,0:T(8,128)(2,1)}, u32[]{:S(2)}, u32[]{:S(2)}) collective-permute-start(bf16[512,512]{1,0:T(8,128)(2,1)S(1)} %collective-permute-done.1.refs_11_), channel_id=1, source_target_pairs={{0,1},{1,2},{2,3},{3,0},{4,5},{5,6},{6,7},{7,4},{8,9},{9,10},{10,1... | collective-permute-start | bytes 1572872 | tf_op jit(solution)/shard_map/ppermute | solution.py:304
  59.3 17.6 %collective-permute-start.11 = (bf16[512,512]{1,0:T(8,128)(2,1)}, bf16[512,512]{1,0:T(8,128)(2,1)}, u32[]{:S(2)}, u32[]{:S(2)}) collective-permute-start(bf16[512,512]{1,0:T(8,128)(2,1)} %collective-permute-done.refs_13_), channel_id=1, source_target_pairs={{0,4},{1,5},{2,6},{3,7},{4,8},{5,9},{6,10},{7,11},{8,12},{9,13},{1... | collective-permute-start | bytes 1572872 | tf_op jit(solution)/shard_map/ppermute | solution.py:308
  59.3 17.6 %collective-permute-start.8 = (bf16[512,512]{1,0:T(8,128)(2,1)}, bf16[512,512]{1,0:T(8,128)(2,1)}, u32[]{:S(2)}, u32[]{:S(2)}) collective-permute-start(bf16[512,512]{1,0:T(8,128)(2,1)} %collective-permute-done.4.refs_15_), channel_id=1, source_target_pairs={{0,3},{1,0},{2,1},{3,2},{4,7},{5,4},{6,5},{7,6},{8,11},{9,8},{10,9... | collective-permute-start | bytes 1572872 | tf_op jit(solution)/shard_map/ppermute | solution.py:304
  61.2 15.6 %collective-permute-start.9 = (bf16[512,512]{1,0:T(8,128)(2,1)}, bf16[512,512]{1,0:T(8,128)(2,1)}, u32[]{:S(2)}, u32[]{:S(2)}) collective-permute-start(bf16[512,512]{1,0:T(8,128)(2,1)} %collective-permute-done.6.refs_17_), channel_id=1, source_target_pairs={{0,12},{1,13},{2,14},{3,15},{4,0},{5,1},{6,2},{7,3},{8,4},{9,5},{1... | collective-permute-start | bytes 1572872 | tf_op jit(solution)/shard_map/ppermute | solution.py:308
  64.6 1.6 %copy-start.8 = (bf16[512,2048]{1,0:T(8,128)(2,1)S(1)}, bf16[512,2048]{1,0:T(8,128)(2,1)}, u32[]{:S(2)}) copy-start(bf16[512,2048]{1,0:T(8,128)(2,1)} %fusion.w_tile.refs_6_) | copy-start | bytes 6291460
  66.2 9.9 %copy-start.12 = (s32[128]{0:T(128)}, s32[128]{0:T(128)S(1)}, u32[]{:S(2)}) copy-start(s32[128]{0:T(128)S(1)} %select_reduce_fusion.refs_2_) | copy-start | bytes 1540
  76.9 29.9 %collective-permute-start.13 = (bf16[512,512]{1,0:T(8,128)(2,1)}, bf16[512,512]{1,0:T(8,128)(2,1)S(1)}, u32[]{:S(2)}, u32[]{:S(2)}) collective-permute-start(bf16[512,512]{1,0:T(8,128)(2,1)} %collective-permute-done.4.refs_15_), channel_id=1, source_target_pairs={{0,12},{1,13},{2,14},{3,15},{4,0},{5,1},{6,2},{7,3},{8,4},{9,5},{1... | collective-permute-start | bytes 1572872 | tf_op jit(solution)/shard_map/ppermute | solution.py:308
  79.0 27.8 %collective-permute-start.12 = (bf16[512,512]{1,0:T(8,128)(2,1)}, bf16[512,512]{1,0:T(8,128)(2,1)S(1)}, u32[]{:S(2)}, u32[]{:S(2)}) collective-permute-start(bf16[512,512]{1,0:T(8,128)(2,1)} %collective-permute-done.5.refs_16_), channel_id=1, source_target_pairs={{0,3},{1,0},{2,1},{3,2},{4,7},{5,4},{6,5},{7,6},{8,11},{9,8},{10,9... | collective-permute-start | bytes 1572872 | tf_op jit(solution)/shard_map/ppermute | solution.py:304
  80.1 26.6 %collective-permute-start.14 = (bf16[512,512]{1,0:T(8,128)(2,1)}, bf16[512,512]{1,0:T(8,128)(2,1)S(1)}, u32[]{:S(2)}, u32[]{:S(2)}) collective-permute-start(bf16[512,512]{1,0:T(8,128)(2,1)} %collective-permute-done.9.refs_20_), channel_id=1, source_target_pairs={{0,1},{1,2},{2,3},{3,0},{4,5},{5,6},{6,7},{7,4},{8,9},{9,10},{10,1... | collective-permute-start | bytes 1572872 | tf_op jit(solution)/shard_map/ppermute | solution.py:304
  81.7 25.1 %copy-start.5 = (s32[17]{0:T(128)S(1)}, s32[17]{0:T(128)}, u32[]{:S(2)}) copy-start(s32[17]{0:T(128)} %stack.75.refs_0_) | copy-start | bytes 208
  (7 other events, 6.5 us)
